TPU v7x, 128 devices: a whole 4x4x4 slice. The times are simulated.
128 devices in a mesh: wave: 16 (over x_lo, z, core), lev: 8 (over x_hi, y).
Axes of the slice: x: 4 (x_hi: 2, x_lo: 2; x = x_hi * 2 + x_lo), y: 4, z: 4, core: 2. Of those that a mesh axis runs over, the one named last changes fastest.
Arguments:
- grid_in: float32 [1, 136, 640, 1280], P(None, 'lev', 'wave'), may hold values from -6 to 6
- wavenumbers: int32 [384], replicated, may hold values from 0 to 383, each once
- legendre: float32 [384, 640, 640], P(('wave', 'lev')), may hold values from -0.25 to 0.25
- modes_in: float32 [136, 136], replicated, may hold values from -0.5 to 0.5
- modes_out: float32 [136, 136], replicated, may hold values from -0.5 to 0.5
- damping: float32 [136], replicated, may hold values from 7.347161e-07 to 7.347161e-05
Outputs:
- grid_out: float32 [1, 136, 640, 1280], P(None, 'lev', 'wave')
Inputs may be any that keep to these rules, and one draw needn't show every extreme that they name: `wavenumbers`: each of 0 to 383 stands once; slot s lies on the device of index s // 3 in the joined wave+lev order.
All inputs are finite; a program needn't handle non-finite values.
Results may differ from a plain program's by a relative error of at most 0.0003.
Values sent between devices are 32-bit elements; how exact they have to be, the bound alone decides.
A program may use at most 128 MiB of HBM per device.

v0:
```python
import math

import jax
import jax.numpy as jnp
from jax import lax
from jax.experimental import pallas as pl
from jax.experimental.pallas import tpu as pltpu
from jax.sharding import PartitionSpec as P

MESH = pl.DeviceIdType.MESH
f32 = jnp.float32
bf16 = jnp.bfloat16

LON = 1280
LAT = 640
COEFF = 640
WAVES = 16
LEVS = 8
DEVS = WAVES * LEVS
LV = 17
LT = 40
SLOTS = 3
LEVELS = LEVS * LV
PAD = 144
ROWS = 16
HALF = DEVS * ROWS
MAIN = 16 * LT // 128


def split(x):
    hi = x.astype(bf16)
    return hi, (x - hi.astype(f32)).astype(bf16)


def dot(a, b, dims):
    return lax.dot_general(a, b, (dims, ((), ())), preferred_element_type=f32)


NN = ((1,), (0,))
NT = ((1,), (1,))


def dot3(ah, al, bh, bl, dims):
    return dot(ah, bh, dims) + dot(al, bh, dims) + dot(ah, bl, dims)


def lanes(rows):
    return lax.broadcasted_iota(jnp.int32, (rows, 128), 1)


def pick(tile, get):
    lane = lanes(8)
    value = None
    for p in range(128 * tile // LT, (128 * tile + 127) // LT + 1):
        value = get(p) if value is None else jnp.where(lane < LT * p - 128 * tile, value, get(p))
    return value


def ring(tiles, shift):
    whole, part = divmod(shift % (128 * MAIN), 128)
    if part == 0:
        return [tiles[(t + whole) % MAIN] for t in range(MAIN)]
    lane = lanes(8)
    rolled = [pltpu.roll(x, 128 - part, 1) for x in tiles]
    return [
        jnp.where(lane < 128 - part, rolled[(t + whole) % MAIN], rolled[(t + whole + 1) % MAIN])
        for t in range(MAIN)
    ]


def kernel(
    waves, damp, modes_f32, cos1, sin1, cos2, sin2, grid, plm, out,
    gf, gh, gl, pf, ph, pw, th, tl, s1, r1, s2, r2, x, e, acc, rth, rtl, modes,
    load_sem, send1, recv1, send2, recv2,
):
    w = lax.axis_index("wave")
    v = lax.axis_index("lev")
    me = w * LEVS + v

    def peer(i):
        t = lax.rem(me + i, DEVS)
        return t, (t // LEVS, lax.rem(t, LEVS))

    for p in range(16):
        pltpu.make_async_copy(
            grid.at[lax.rem(p - w + 16, 16)], gf.at[pl.ds(LT * p, LT)], load_sem.at[0]
        ).start()
    for s in range(SLOTS):
        pltpu.make_async_copy(
            grid.at[16], gf.at[pl.ds(16 * LT + LT * s, LT)], load_sem.at[0]
        ).start()
    for s in range(SLOTS):
        pltpu.make_async_copy(plm.at[s], pf.at[pl.ds(LAT * s, LAT)], load_sem.at[1]).start()

    barrier = pltpu.get_barrier_semaphore()

    def greet(i, carry):
        pl.semaphore_signal(barrier, inc=1, device_id=peer(i)[1], device_id_type=MESH)
        return carry

    lax.fori_loop(1, DEVS, greet, 0)

    def table(i, carry):
        rows = pl.ds(pl.multiple_of(32 * i, 32), 32)
        rows_sin = pl.ds(pl.multiple_of(32 * i + 384, 32), 32)
        c1, n1 = cos1[rows, :], sin1[rows, :]
        c2, n2 = cos2[rows, :], sin2[rows, :]
        for a in range(LON // 128):
            ca, sa = c2[:, a : a + 1], n2[:, a : a + 1]
            col = slice(128 * a, 128 * a + 128)
            hi, lo = split(c1 * ca - n1 * sa)
            th[rows, col] = hi
            tl[rows, col] = lo
            hi, lo = split(-(n1 * ca + c1 * sa))
            th[rows_sin, col] = hi
            tl[rows_sin, col] = lo
        return carry

    lax.fori_loop(0, 12, table, 0)

    pltpu.make_async_copy(gf.at[pl.ds(0, 760)], gf.at[pl.ds(0, 760)], load_sem.at[0]).wait()
    gf[760:768, :] = jnp.zeros((8, LON), f32)

    def split_grid(i, carry):
        rows = pl.ds(pl.multiple_of(32 * i, 32), 32)
        gh[rows, :], gl[rows, :] = split(gf[rows, :])
        return carry

    lax.fori_loop(0, 24, split_grid, 0)

    lane128 = lanes(128)

    def forward_dft(c):
        def step(n, carry):
            cols = pl.ds(pl.multiple_of(256 * n, 256), 256)
            part = slice(384 * c, 384 * c + 384)
            y = dot3(th[part, :], tl[part, :], gh[cols, :], gl[cols, :], NT)
            for h in range(2):
                yh = y[:, 128 * h : 128 * h + 128]

                def main():
                    for s in range(SLOTS):
                        start = HALF * c + MAIN * s + 2 * n + h
                        s1[pl.ds(start, DEVS, ROWS), :] = yh[128 * s : 128 * s + 128]

                if h == 0:
                    main()
                else:
                    pl.when(n < 2)(main)

                    @pl.when(n == 2)
                    def _():
                        last = jnp.where(
                            lane128 < LT,
                            yh[0:128],
                            jnp.where(lane128 < 2 * LT, yh[128:256], yh[256:384]),
                        )
                        s1[pl.ds(HALF * c + ROWS - 1, DEVS, ROWS), :] = last

            return carry

        lax.fori_loop(0, 3, step, 0)

    def block(c, d):
        return pl.ds(pl.multiple_of((c * DEVS + d) * ROWS, ROWS), ROWS)

    def send(c, src, dst, send_sem, recv_sem):
        pltpu.make_async_copy(src.at[block(c, me)], dst.at[block(c, me)], recv_sem.at[c]).start()

        def go(i, carry):
            t, where = peer(i)
            pltpu.make_async_remote_copy(
                src_ref=src.at[block(c, t)],
                dst_ref=dst.at[block(c, me)],
                send_sem=send_sem.at[c],
                recv_sem=recv_sem.at[c],
                device_id=where,
                device_id_type=MESH,
            ).start()
            return carry

        lax.fori_loop(1, DEVS, go, 0)

    def arrive(c, dst, recv_sem):
        half = dst.at[pl.ds(HALF * c, HALF)]
        pltpu.make_async_copy(half, half, recv_sem.at[c]).wait()

    def sent(c, src, send_sem):
        part = src.at[pl.ds(0, HALF - ROWS)]
        pltpu.make_async_copy(part, part, send_sem.at[c]).wait()

    forward_dft(0)
    pl.semaphore_wait(barrier, DEVS - 1)
    send(0, s1, r1, send1, recv1)
    forward_dft(1)
    send(1, s1, r1, send1, recv1)

    pltpu.make_async_copy(pf, pf, load_sem.at[1]).wait()

    def split_plm(i, carry):
        rows = pl.ds(pl.multiple_of(64 * i, 64), 64)
        ph[rows, :], pw[rows, :] = split(pf[rows, :])
        return carry

    lax.fori_loop(0, SLOTS * LAT // 64, split_plm, 0)

    modes[0], modes[1] = split(modes_f32[0])
    modes[2], modes[3] = split(modes_f32[1])
    x[LEVELS:PAD, :] = jnp.zeros((PAD - LEVELS, LAT), f32)
    lane8 = lanes(8)

    def middle(c):
        acc[...] = jnp.zeros((WAVES * 8, 128), f32)

        def slot(s, carry):
            base = HALF * c + MAIN * s
            for k in range(16):
                tiles = [
                    pick(t, lambda p: r1[pl.ds(base + ((p - k) % 16) * 128 + t, 8, ROWS), :])
                    for t in range(MAIN)
                ]
                for t, value in enumerate(ring(tiles, LT * k)):
                    x[8 * k : 8 * k + 8, 128 * t : 128 * t + 128] = value
            tiles = [None] * MAIN
            for q in range(WAVES):
                own = r1[pl.ds(HALF * c + q * 128 + ROWS - 1, 8, ROWS), :]
                own = pltpu.roll(own, lax.rem(LT * q - LT * s + 768, 128), 1)
                t, off = divmod(LT * q, 128)
                tiles[t] = own if off == 0 else jnp.where(lane8 < off, tiles[t], own)
                if off + LT > 128:
                    tiles[t + 1] = own
            for t in range(MAIN):
                x[128:136, 128 * t : 128 * t + 128] = tiles[t]

            prow = pl.ds(pl.multiple_of(LAT * s, LAT), LAT)
            xh, xl = split(x[...])
            spec = dot3(xh, xl, ph[prow, :], pw[prow, :], NN)
            degree = waves[SLOTS * me + s] + lax.broadcasted_iota(jnp.int32, (PAD, COEFF), 1)
            growth = (degree * (degree + 1)).astype(f32)
            factor = jnp.where(degree < COEFF, 1.0 / (1.0 + damp[...] * growth), 0.0)
            sh, sl = split(spec)
            modal = dot3(modes[0], modes[1], sh, sl, NN) * factor
            mh, ml = split(modal)
            solved = dot3(modes[2], modes[3], mh, ml, NN)
            vh, vl = split(solved)
            x[...] = dot3(vh, vl, ph[prow, :], pw[prow, :], NT)

            for k in range(16):
                tiles = [x[8 * k : 8 * k + 8, 128 * t : 128 * t + 128] for t in range(MAIN)]
                for t, value in enumerate(ring(tiles, -LT * k)):
                    e[8 * k : 8 * k + 8, 128 * t : 128 * t + 128] = value
            for q in range(WAVES):
                for t in range(MAIN):

                    def get(p):
                        k = (p - q) % 16
                        return e[8 * k : 8 * k + 8, 128 * t : 128 * t + 128]

                    s2[pl.ds(base + q * 128 + t, 8, ROWS), :] = pick(t, get)
                t, off = divmod(LT * q, 128)
                own = x[128:136, 128 * t : 128 * t + 128]
                if off + LT > 128:
                    after = x[128:136, 128 * t + 128 : 128 * t + 256]
                    own = jnp.where(lane8 < off, after, own)
                own = pltpu.roll(own, lax.rem(LT * s - LT * q + 768, 128), 1)
                inside = (lane8 >= LT * s) & (lane8 < LT * s + LT)
                acc[8 * q : 8 * q + 8, :] = jnp.where(inside, own, acc[8 * q : 8 * q + 8, :])
            return carry

        lax.fori_loop(0, SLOTS, slot, 0)
        s2[pl.ds(HALF * c + ROWS - 1, DEVS, ROWS), :] = acc[...]

    for c in range(2):
        arrive(c, r1, recv1)
        middle(c)
        send(c, s2, r2, send2, recv2)

    def adjoint_dft(c):
        for s in range(SLOTS):
            for t in range(MAIN):
                tile = r2[pl.ds(HALF * c + MAIN * s + t, DEVS, ROWS), :]
                hi, lo = split(tile.T)
                rth[128 * t : 128 * t + 128, 128 * s : 128 * s + 128] = hi
                rtl[128 * t : 128 * t + 128, 128 * s : 128 * s + 128] = lo
            tile = r2[pl.ds(HALF * c + ROWS - 1, DEVS, ROWS), :]
            inside = (lane128 >= LT * s) & (lane128 < LT * s + LT)
            hi, lo = split(jnp.where(inside, tile, 0.0).T)
            rth[128 * MAIN :, 128 * s : 128 * s + 128] = hi
            rtl[128 * MAIN :, 128 * s : 128 * s + 128] = lo

        def step(n, carry):
            cols = pl.ds(pl.multiple_of(256 * n, 256), 256)
            part = slice(384 * c, 384 * c + 384)
            y = dot3(rth[...], rtl[...], th[part, cols], tl[part, cols], NN)
            if c == 0:
                gf[:, cols] = y
            else:
                gf[:, cols] += y
            return carry

        lax.fori_loop(0, LON // 256, step, 0)

    for c in range(2):
        arrive(c, r2, recv2)
        adjoint_dft(c)

    gf[640:680, :] = gf[640:680, :] + gf[680:720, :] + gf[720:760, :]
    for p in range(17):
        level = lax.rem(p - w + 16, 16) if p < 16 else 16
        pltpu.make_async_copy(gf.at[pl.ds(LT * p, LT)], out.at[level], load_sem.at[2]).start()
    for c in range(2):
        sent(c, s1, send1)
        sent(c, s2, send2)
    done = gf.at[pl.ds(0, 680)]
    pltpu.make_async_copy(done, done, load_sem.at[2]).wait()


def tables(wavenumbers):
    order = wavenumbers.reshape(DEVS, SLOTS).T.reshape(DEVS * SLOTS, 1)
    near = order * jnp.arange(128, dtype=jnp.int32)[None, :] % LON
    far = order * jnp.arange(16, dtype=jnp.int32)[None, :] % (LON // 128)
    near = near.astype(f32) * (2.0 * math.pi / LON)
    far = far.astype(f32) * (2.0 * math.pi / (LON // 128))
    scale = 1.0 / math.sqrt(LON)
    return jnp.cos(near) * scale, jnp.sin(near) * scale, jnp.cos(far), jnp.sin(far)


def local(grid_in, wavenumbers, legendre, modes_in, modes_out, damping):
    grid = grid_in.reshape(LV, LT, LON)
    m_in = modes_in.reshape(LEVELS, LEVS, LV).transpose(0, 2, 1).reshape(LEVELS, LEVELS)
    m_out = modes_out.reshape(LEVS, LV, LEVELS).transpose(1, 0, 2).reshape(LEVELS, LEVELS)
    pad = PAD - LEVELS
    modes = jnp.pad(jnp.stack([m_in, m_out]), ((0, 0), (0, pad), (0, pad)))
    damp = jnp.pad(damping, (0, pad)).reshape(PAD, 1)
    vmem = pl.BlockSpec(memory_space=pltpu.VMEM)
    hbm = pl.BlockSpec(memory_space=pl.ANY)
    dma = pltpu.SemaphoreType.DMA
    result = pl.pallas_call(
        kernel,
        out_shape=jax.ShapeDtypeStruct((LV, LT, LON), f32),
        in_specs=[pl.BlockSpec(memory_space=pltpu.SMEM)] + [vmem] * 6 + [hbm] * 2,
        out_specs=hbm,
        scratch_shapes=[
            pltpu.VMEM((768, LON), f32),
            pltpu.VMEM((768, LON), bf16),
            pltpu.VMEM((768, LON), bf16),
            pltpu.VMEM((SLOTS * LAT, COEFF), f32),
            pltpu.VMEM((SLOTS * LAT, COEFF), bf16),
            pltpu.VMEM((SLOTS * LAT, COEFF), bf16),
            pltpu.VMEM((768, LON), bf16),
            pltpu.VMEM((768, LON), bf16),
            pltpu.VMEM((2 * HALF, 128), f32),
            pltpu.VMEM((2 * HALF, 128), f32),
            pltpu.VMEM((2 * HALF, 128), f32),
            pltpu.VMEM((2 * HALF, 128), f32),
            pltpu.VMEM((PAD, LAT), f32),
            pltpu.VMEM((128, LAT), f32),
            pltpu.VMEM((WAVES * 8, 128), f32),
            pltpu.VMEM((768, 384), bf16),
            pltpu.VMEM((768, 384), bf16),
            pltpu.VMEM((4, PAD, PAD), bf16),
            dma((3,)),
            dma((2,)),
            dma((2,)),
            dma((2,)),
            dma((2,)),
        ],
        compiler_params=pltpu.CompilerParams(
            collective_id=0, has_side_effects=True, vmem_limit_bytes=56 << 20
        ),
        name="spectral_step",
    )(wavenumbers, damp, modes, *tables(wavenumbers), grid, legendre)
    return result.reshape(1, LV, LT, LON)


def solution(mesh):
    return jax.shard_map(
        local,
        mesh=mesh,
        in_specs=(P(None, "lev", "wave", None), P(), P(("wave", "lev"), None, None), P(), P(), P()),
        out_specs=P(None, "lev", "wave", None),
        check_vma=False,
    )
```

profile of v0, /device:TPU:1, one launch (start us, length us, event | category | flops | bytes accessed | tf_op | source)
XLA Modules:
  0.0 93.7 jit_solution(2397665201777358092)
XLA Ops:
  0.0 0.7 pad.8
  0.7 0.9 reshape.23
  1.6 0.1 copy.19
  1.7 0.7 copy.21.damp
  2.4 1.0 %copy.15 = f32[136,136]{0,1:T(8,128)S(1)} copy(f32[136,136]{1,0:T(8,128)} %param.9) | data formatting | bytes 147968 | tf_op args[3]
  3.5 0.1 copy.18
  3.6 0.1 copy.20
  3.8 0.9 reshape.22
  4.7 0.7 select_maximum_fusion.modes_f32
  5.5 1.4 %multiply_sine_fusion = (f32[384,16]{1,0:T(8,128)}, f32[384,16]{1,0:T(8,128)}) fusion(f32[384,16]{1,0:T(8,128)S(1)} %copy.20), kind=kLoop, calls=%fused_computation.12 | loop fusion | flops 6144 | bytes 73728 | tf_op jit(solution)/shard_map/sin | solution.py:325
  6.9 1.7 %sine_multiply_fusion = (f32[384,128]{1,0:T(8,128)}, f32[384,128]{1,0:T(8,128)}) fusion(s32[384]{0:T(512)S(1)} %bitcast.23), kind=kLoop, calls=%fused_computation.6 | loop fusion | flops 540672 | bytes 394752 | tf_op jit(solution)/shard_map/mul | solution.py:325
  8.6 81.1 %spectral_step.1 = f32[17,40,1280]{2,1,0:T(8,128)} custom-call(s32[384]{0:T(512)} %waves.1, f32[144,1]{1,0:T(8,128)} %copy.21.damp, f32[2,144,144]{2,1,0:T(8,128)} %select_maximum_fusion.modes_f32, f32[384,128]{1,0:T(8,128)} %get-tuple-element.8.cos1, f32[384,128]{1,0:T(8,128)} %get-tuple-element.7.sin1, f32[384,16]{1,0:T(8,128)} %get-tuple-element.6.cos2, ...), custom_call_target="tpu_custom_call" | custom-call | tf_op jit(solution)/shard_map/spectral_step/pallas_call | solution.py:338
  89.7 4.0 %copy.27 = f32[1,17,40,1280]{3,2,1,0:T(8,128)} copy(f32[1,17,40,1280]{3,2,1,0:T(8,128)} %bitcast.15) | data formatting | bytes 6963200
  (4 shorter events, 0.2 us)
where the time goes:
time: 93.9 us; the launch traced here: 93.7 us
  Pallas kernels  81.1 us (86%)
  local copies, waits for them, and re-layouts  8.61 us (9%)
  other arithmetic  3.91 us (4%)
    pallas_call x1, Pallas kernels, local(): pl.pallas_call(kernel, out_shape=jax.ShapeDtypeStruct((LV, LT, LON), f32)...  81.1 us
    unnamed x2, local copies, waits for them, and re-layouts  4.99 us

commit v1 on v0

--- a/solution.py
+++ b/solution.py
@@ -2,6 +2,7 @@
 
 import jax
 import jax.numpy as jnp
+import numpy as np
 from jax import lax
 from jax.experimental import pallas as pl
 from jax.experimental.pallas import tpu as pltpu
@@ -36,6 +37,7 @@
     return lax.dot_general(a, b, (dims, ((), ())), preferred_element_type=f32)
 
 
+TN = ((0,), (0,))
 NN = ((1,), (0,))
 NT = ((1,), (1,))
 
@@ -68,19 +70,53 @@
     ]
 
 
+def coordinates():
+    w = lax.axis_index("wave")
+    v = lax.axis_index("lev")
+    return 2 * (v // 4) + w // 8, lax.rem(v, 4), lax.rem(w // 2, 4), lax.rem(w, 2)
+
+
+def each_peer(visit):
+    x, y, z, core = coordinates()
+    xs = [lax.rem(x + a, 4) for a in range(4)]
+    wave_x = [8 * lax.rem(a, 2) for a in xs]
+    lev_x = [4 * (a // 2) for a in xs]
+    lev_y = [lax.rem(y + b, 4) for b in range(4)]
+
+    def outer(j, carry):
+        wave_c = lax.rem(core + j // 4, 2)
+        wave_z = [2 * lax.rem(z + j + d, 4) + wave_c for d in range(4)]
+        for i in range(1, 16):
+            a, b = i % 4, i // 4
+            visit(wave_x[a] + wave_z[(b + 2 * a) % 4], lev_x[a] + lev_y[(a + b) % 4])
+        return carry
+
+    lax.fori_loop(0, 8, outer, 0)
+    for j in range(1, 8):
+        visit(wave_x[0] + 2 * lax.rem(z + j, 4) + lax.rem(core + j // 4, 2), lev_x[0] + lev_y[0])
+
+
 def kernel(
-    waves, damp, modes_f32, cos1, sin1, cos2, sin2, grid, plm, out,
-    gf, gh, gl, pf, ph, pw, th, tl, s1, r1, s2, r2, x, e, acc, rth, rtl, modes,
+    waves, waves_row, damp_row, circle, modes_in, modes_out, order, order_t, grid, plm,
+    gf, th, tl, rth, rtl,
+    gh, gl, pf, ph, pw, s1, r1, s2, r2, x, e, acc, modes, damp,
+    circle_v, min_v, mout_v, order_v, order_tv, near_cos, near_sin, far,
     load_sem, send1, recv1, send2, recv2,
 ):
     w = lax.axis_index("wave")
     v = lax.axis_index("lev")
     me = w * LEVS + v
 
-    def peer(i):
-        t = lax.rem(me + i, DEVS)
-        return t, (t // LEVS, lax.rem(t, LEVS))
-
+    small = [
+        pltpu.make_async_copy(a, b, load_sem.at[2 + i])
+        for i, (a, b) in enumerate(
+            [
+                (circle, circle_v), (modes_in, min_v), (modes_out, mout_v),
+                (order, order_v), (order_t, order_tv),
+            ]
+        )
+    ]
+    small[0].start()
     for p in range(16):
         pltpu.make_async_copy(
             grid.at[lax.rem(p - w + 16, 16)], gf.at[pl.ds(LT * p, LT)], load_sem.at[0]
@@ -89,34 +125,55 @@
         pltpu.make_async_copy(
             grid.at[16], gf.at[pl.ds(16 * LT + LT * s, LT)], load_sem.at[0]
         ).start()
+
+    barrier = pltpu.get_barrier_semaphore()
+
+    def greet(to_wave, to_lev):
+        pl.semaphore_signal(barrier, inc=1, device_id=(to_wave, to_lev), device_id_type=MESH)
+
+    each_peer(greet)
+    for copy in small[1:]:
+        copy.start()
     for s in range(SLOTS):
         pltpu.make_async_copy(plm.at[s], pf.at[pl.ds(LAT * s, LAT)], load_sem.at[1]).start()
 
-    barrier = pltpu.get_barrier_semaphore()
-
-    def greet(i, carry):
-        pl.semaphore_signal(barrier, inc=1, device_id=peer(i)[1], device_id_type=MESH)
-        return carry
-
-    lax.fori_loop(1, DEVS, greet, 0)
-
-    def table(i, carry):
-        rows = pl.ds(pl.multiple_of(32 * i, 32), 32)
-        rows_sin = pl.ds(pl.multiple_of(32 * i + 384, 32), 32)
-        c1, n1 = cos1[rows, :], sin1[rows, :]
-        c2, n2 = cos2[rows, :], sin2[rows, :]
-        for a in range(LON // 128):
-            ca, sa = c2[:, a : a + 1], n2[:, a : a + 1]
-            col = slice(128 * a, 128 * a + 128)
-            hi, lo = split(c1 * ca - n1 * sa)
-            th[rows, col] = hi
-            tl[rows, col] = lo
-            hi, lo = split(-(n1 * ca + c1 * sa))
-            th[rows_sin, col] = hi
-            tl[rows_sin, col] = lo
-        return carry
-
-    lax.fori_loop(0, 12, table, 0)
+    slots = DEVS * SLOTS
+    eye = lax.broadcasted_iota(jnp.int32, (slots, slots), 0) == lax.broadcasted_iota(
+        jnp.int32, (slots, slots), 1
+    )
+    column = jnp.sum(
+        jnp.where(eye, waves_row[...].astype(f32), 0.0), axis=1, keepdims=True
+    ).astype(jnp.int32)
+    chosen = (lax.broadcasted_iota(jnp.int32, (slots, slots), 1) == column).astype(bf16)
+    small[0].wait()
+    rest = circle_v[...]
+    top, _ = split(rest)
+    rest = rest - top.astype(f32)
+    mid, low = split(rest)
+    rows3 = dot(chosen, top, NN) + dot(chosen, mid, NN) + dot(chosen, low, NN)
+    near_cos[...] = rows3[:, 0:128]
+    near_sin[...] = rows3[:, 128:256]
+    far[...] = rows3[:, 256:384]
+
+    for s in range(SLOTS):
+
+        def table(i, carry):
+            mine = pl.ds(s + 96 * i, 32, SLOTS)
+            rows = pl.ds(pl.multiple_of(32 * i + 128 * s, 32), 32)
+            rows_sin = pl.ds(pl.multiple_of(32 * i + 128 * s + 384, 32), 32)
+            c1, n1, f = near_cos[mine, :], near_sin[mine, :], far[mine, :]
+            for a in range(LON // 128):
+                ca, sa = f[:, a : a + 1], f[:, 16 + a : 17 + a]
+                col = slice(128 * a, 128 * a + 128)
+                hi, lo = split(c1 * ca - n1 * sa)
+                th[rows, col] = hi
+                tl[rows, col] = lo
+                hi, lo = split(-(n1 * ca + c1 * sa))
+                th[rows_sin, col] = hi
+                tl[rows_sin, col] = lo
+            return carry
+
+        lax.fori_loop(0, 4, table, 0)
 
     pltpu.make_async_copy(gf.at[pl.ds(0, 760)], gf.at[pl.ds(0, 760)], load_sem.at[0]).wait()
     gf[760:768, :] = jnp.zeros((8, LON), f32)
@@ -167,19 +224,17 @@
     def send(c, src, dst, send_sem, recv_sem):
         pltpu.make_async_copy(src.at[block(c, me)], dst.at[block(c, me)], recv_sem.at[c]).start()
 
-        def go(i, carry):
-            t, where = peer(i)
+        def go(to_wave, to_lev):
             pltpu.make_async_remote_copy(
-                src_ref=src.at[block(c, t)],
+                src_ref=src.at[block(c, to_wave * LEVS + to_lev)],
                 dst_ref=dst.at[block(c, me)],
                 send_sem=send_sem.at[c],
                 recv_sem=recv_sem.at[c],
-                device_id=where,
+                device_id=(to_wave, to_lev),
                 device_id_type=MESH,
             ).start()
-            return carry
-
-        lax.fori_loop(1, DEVS, go, 0)
+
+        each_peer(go)
 
     def arrive(c, dst, recv_sem):
         half = dst.at[pl.ds(HALF * c, HALF)]
@@ -204,8 +259,17 @@
 
     lax.fori_loop(0, SLOTS * LAT // 64, split_plm, 0)
 
-    modes[0], modes[1] = split(modes_f32[0])
-    modes[2], modes[3] = split(modes_f32[1])
+    for copy in small[1:]:
+        copy.wait()
+    pad = PAD - LEVELS
+    for i, part in enumerate(split(jnp.concatenate([min_v[...], jnp.zeros((pad, LEVELS), f32)], 0))):
+        modes[i] = dot(part, order_v[...].astype(bf16), NN).astype(bf16)
+    for i, part in enumerate(split(jnp.concatenate([mout_v[...], jnp.zeros((LEVELS, pad), f32)], 1))):
+        modes[2 + i] = dot(order_tv[...].astype(bf16), part, NN).astype(bf16)
+    eye = lax.broadcasted_iota(jnp.int32, (PAD, LEVELS), 0) == lax.broadcasted_iota(
+        jnp.int32, (PAD, LEVELS), 1
+    )
+    damp[...] = jnp.sum(jnp.where(eye, damp_row[...], 0.0), axis=1, keepdims=True)
     x[LEVELS:PAD, :] = jnp.zeros((PAD - LEVELS, LAT), f32)
     lane8 = lanes(8)
 
@@ -275,7 +339,7 @@
         middle(c)
         send(c, s2, r2, send2, recv2)
 
-    def adjoint_dft(c):
+    def transpose(c):
         for s in range(SLOTS):
             for t in range(MAIN):
                 tile = r2[pl.ds(HALF * c + MAIN * s + t, DEVS, ROWS), :]
@@ -288,67 +352,80 @@
             rth[128 * MAIN :, 128 * s : 128 * s + 128] = hi
             rtl[128 * MAIN :, 128 * s : 128 * s + 128] = lo
 
-        def step(n, carry):
-            cols = pl.ds(pl.multiple_of(256 * n, 256), 256)
-            part = slice(384 * c, 384 * c + 384)
-            y = dot3(rth[...], rtl[...], th[part, cols], tl[part, cols], NN)
-            if c == 0:
-                gf[:, cols] = y
-            else:
-                gf[:, cols] += y
-            return carry
-
-        lax.fori_loop(0, LON // 256, step, 0)
-
-    for c in range(2):
-        arrive(c, r2, recv2)
-        adjoint_dft(c)
-
-    gf[640:680, :] = gf[640:680, :] + gf[680:720, :] + gf[720:760, :]
-    for p in range(17):
-        level = lax.rem(p - w + 16, 16) if p < 16 else 16
-        pltpu.make_async_copy(gf.at[pl.ds(LT * p, LT)], out.at[level], load_sem.at[2]).start()
+    arrive(0, r2, recv2)
+    transpose(0)
+
+    def adjoint(n, carry):
+        cols = pl.ds(pl.multiple_of(256 * n, 256), 256)
+        gf[:, cols] = dot3(rth[...], rtl[...], th[0:384, cols], tl[0:384, cols], NN)
+        return carry
+
+    lax.fori_loop(0, LON // 256, adjoint, 0)
     for c in range(2):
         sent(c, s1, send1)
         sent(c, s2, send2)
-    done = gf.at[pl.ds(0, 680)]
-    pltpu.make_async_copy(done, done, load_sem.at[2]).wait()
-
-
-def tables(wavenumbers):
-    order = wavenumbers.reshape(DEVS, SLOTS).T.reshape(DEVS * SLOTS, 1)
-    near = order * jnp.arange(128, dtype=jnp.int32)[None, :] % LON
-    far = order * jnp.arange(16, dtype=jnp.int32)[None, :] % (LON // 128)
-    near = near.astype(f32) * (2.0 * math.pi / LON)
-    far = far.astype(f32) * (2.0 * math.pi / (LON // 128))
-    scale = 1.0 / math.sqrt(LON)
-    return jnp.cos(near) * scale, jnp.sin(near) * scale, jnp.cos(far), jnp.sin(far)
+    arrive(1, r2, recv2)
+    transpose(1)
+
+
+def finish(gf, th, tl, rth, rtl, out, block, sem):
+    w = lax.axis_index("wave")
+    copies = []
+    for n in range(LON // 256):
+        cols = slice(256 * n, 256 * n + 256)
+        y = gf[:, cols] + dot3(rth[...], rtl[...], th[384:768, cols], tl[384:768, cols], NN)
+        for p in range(16):
+            level = lax.rem(p - w + 16, 16)
+            block[n, pl.ds(pl.multiple_of(LT * level, 8), LT), :] = y[LT * p : LT * p + LT]
+        block[n, 640:680, :] = y[640:680] + y[680:720] + y[720:760]
+        copy = pltpu.make_async_copy(block.at[n], out.at[:, cols], sem.at[n])
+        copy.start()
+        copies.append(copy)
+    for copy in copies:
+        copy.wait()
+
+
+def circle_table():
+    wave = np.arange(DEVS * SLOTS)[:, None]
+    near = 2.0 * math.pi / LON * (wave * np.arange(128)[None, :] % LON)
+    far = 2.0 * math.pi / 10 * (wave * np.arange(16)[None, :] % 10)
+    table = np.zeros((DEVS * SLOTS, 384))
+    table[:, :128] = np.cos(near) / math.sqrt(LON)
+    table[:, 128:256] = np.sin(near) / math.sqrt(LON)
+    table[:, 256:272] = np.cos(far)
+    table[:, 272:288] = np.sin(far)
+    return table.astype(np.float32)
+
+
+def level_order():
+    matrix = np.zeros((LEVELS, PAD), np.float32)
+    level = np.arange(LEVELS)
+    matrix[level, level % LV * LEVS + level // LV] = 1
+    return matrix
 
 
 def local(grid_in, wavenumbers, legendre, modes_in, modes_out, damping):
-    grid = grid_in.reshape(LV, LT, LON)
-    m_in = modes_in.reshape(LEVELS, LEVS, LV).transpose(0, 2, 1).reshape(LEVELS, LEVELS)
-    m_out = modes_out.reshape(LEVS, LV, LEVELS).transpose(1, 0, 2).reshape(LEVELS, LEVELS)
-    pad = PAD - LEVELS
-    modes = jnp.pad(jnp.stack([m_in, m_out]), ((0, 0), (0, pad), (0, pad)))
-    damp = jnp.pad(damping, (0, pad)).reshape(PAD, 1)
+    order = level_order()
     vmem = pl.BlockSpec(memory_space=pltpu.VMEM)
     hbm = pl.BlockSpec(memory_space=pl.ANY)
     dma = pltpu.SemaphoreType.DMA
-    result = pl.pallas_call(
+    held = pl.pallas_call(
         kernel,
-        out_shape=jax.ShapeDtypeStruct((LV, LT, LON), f32),
-        in_specs=[pl.BlockSpec(memory_space=pltpu.SMEM)] + [vmem] * 6 + [hbm] * 2,
-        out_specs=hbm,
+        out_shape=[
+            pltpu.VMEM((768, LON), f32),
+            pltpu.VMEM((768, LON), bf16),
+            pltpu.VMEM((768, LON), bf16),
+            pltpu.VMEM((768, 384), bf16),
+            pltpu.VMEM((768, 384), bf16),
+        ],
+        in_specs=[pl.BlockSpec(memory_space=pltpu.SMEM)] + [vmem] * 2 + [hbm] * 7,
+        out_specs=[vmem] * 5,
         scratch_shapes=[
-            pltpu.VMEM((768, LON), f32),
             pltpu.VMEM((768, LON), bf16),
             pltpu.VMEM((768, LON), bf16),
             pltpu.VMEM((SLOTS * LAT, COEFF), f32),
             pltpu.VMEM((SLOTS * LAT, COEFF), bf16),
             pltpu.VMEM((SLOTS * LAT, COEFF), bf16),
-            pltpu.VMEM((768, LON), bf16),
-            pltpu.VMEM((768, LON), bf16),
             pltpu.VMEM((2 * HALF, 128), f32),
             pltpu.VMEM((2 * HALF, 128), f32),
             pltpu.VMEM((2 * HALF, 128), f32),
@@ -356,20 +433,43 @@
             pltpu.VMEM((PAD, LAT), f32),
             pltpu.VMEM((128, LAT), f32),
             pltpu.VMEM((WAVES * 8, 128), f32),
-            pltpu.VMEM((768, 384), bf16),
-            pltpu.VMEM((768, 384), bf16),
             pltpu.VMEM((4, PAD, PAD), bf16),
-            dma((3,)),
+            pltpu.VMEM((PAD, 1), f32),
+            pltpu.VMEM((DEVS * SLOTS, 384), f32),
+            pltpu.VMEM((LEVELS, LEVELS), f32),
+            pltpu.VMEM((LEVELS, LEVELS), f32),
+            pltpu.VMEM((LEVELS, PAD), f32),
+            pltpu.VMEM((PAD, LEVELS), f32),
+            pltpu.VMEM((DEVS * SLOTS, 128), f32),
+            pltpu.VMEM((DEVS * SLOTS, 128), f32),
+            pltpu.VMEM((DEVS * SLOTS, 128), f32),
+            dma((7,)),
             dma((2,)),
             dma((2,)),
             dma((2,)),
             dma((2,)),
         ],
         compiler_params=pltpu.CompilerParams(
-            collective_id=0, has_side_effects=True, vmem_limit_bytes=56 << 20
+            collective_id=0, has_side_effects=True, vmem_limit_bytes=48 << 20
         ),
         name="spectral_step",
-    )(wavenumbers, damp, modes, *tables(wavenumbers), grid, legendre)
+    )(
+        wavenumbers, wavenumbers.reshape(1, -1), damping.reshape(1, -1), jnp.asarray(circle_table()),
+        modes_in, modes_out, jnp.asarray(order), jnp.asarray(order.T.copy()),
+        grid_in.reshape(LV, LT, LON), legendre,
+    )
+    result = pl.pallas_call(
+        finish,
+        out_shape=jax.ShapeDtypeStruct((LV * LT, LON), f32),
+        in_specs=[vmem] * 5,
+        out_specs=hbm,
+        scratch_shapes=[
+            pltpu.VMEM((LON // 256, LV * LT, 256), f32),
+            dma((LON // 256,)),
+        ],
+        compiler_params=pltpu.CompilerParams(vmem_limit_bytes=40 << 20),
+        name="finish",
+    )(*[pltpu.with_memory_space_constraint(a, pltpu.VMEM) for a in held])
     return result.reshape(1, LV, LT, LON)
 
 

time: 93.9 us -> 70.3 us (0.75)
  Pallas kernels: 81.1 us -> 68.9 us
  local copies, waits for them, and re-layouts: 8.61 us -> 1.24 us
  other arithmetic: 3.91 us -> 0 us
    pallas_call x1 -> x2, Pallas kernels: 81.1 us -> 68.9 us  [the longest x1 64.7 us: local(): pl.pallas_call(kernel, out_shape=[pltpu.VMEM((768, LON), f32), pltpu.VMEM...]
    unnamed x2 -> x0, local copies, waits for them, and re-layouts: 4.99 us -> none
    mul x1 -> x0, other arithmetic: 1.68 us -> none  [tables(): jnp.sin(near) * scale]
    sin x1 -> x0, other arithmetic: 1.45 us -> none  [tables(): jnp.sin(far)]
    reshape x4 -> x1, local copies, waits for them, and re-layouts: 2.57 us -> 1.24 us  [local(): wavenumbers.reshape(1, -1)]
where the time goes in v1:
time: 70.3 us; the launch traced here: 70.1 us
  Pallas kernels  68.9 us (98%)
  local copies, waits for them, and re-layouts  1.24 us (2%)
    pallas_call x1, Pallas kernels, local(): pl.pallas_call(kernel, out_shape=[pltpu.VMEM((768, LON), f32), pltpu.VMEM...  64.7 us
    pallas_call x1, Pallas kernels, local(): pl.pallas_call(finish, out_shape=jax.ShapeDtypeStruct((LV * LT, LON), f32...  4.18 us

profile of v1, /device:TPU:1, one launch (start us, length us, event | category | flops | bytes accessed | tf_op | source)
XLA Modules:
  0.0 70.1 jit_solution(574279805406773078)
XLA Ops:
  0.0 1.2 %reshape.12.waves_row = s32[1,384]{1,0:T(1,128)} reshape(s32[384]{0:T(512)} %waves.1) | data formatting | bytes 3072 | tf_op jit(solution)/shard_map/reshape | solution.py:457
  1.2 64.7 %spectral_step.1 = (f32[768,1280]{1,0:T(8,128)S(1)}, bf16[768,1280]{1,0:T(8,128)(2,1)S(1)}, bf16[768,1280]{1,0:T(8,128)(2,1)S(1)}, bf16[768,384]{1,0:T(8,128)(2,1)S(1)}, bf16[768,384]{1,0:T(8,128)(2,1)S(1)}) custom-call(s32[384]{0:T(512)} %waves.1, s32[1,384]{1,0:T(1,128)} %reshape.12.waves_row, f32[1,136]{1,0:T(1,128)} %bitcast.4, ...), custom_call_target="tpu_custom_call" | custom-call | tf_op jit(solution)/shard_map/spectral_step/pallas_call | solution.py:412
  65.9 4.2 %finish.1 = f32[680,1280]{1,0:T(8,128)} custom-call(f32[768,1280]{1,0:T(8,128)S(1)} %get-tuple-element.10.gf, bf16[768,1280]{1,0:T(8,128)(2,1)S(1)} %get-tuple-element.11.th, bf16[768,1280]{1,0:T(8,128)(2,1)S(1)} %get-tuple-element.12.tl, bf16[768,384]{1,0:T(8,128)(2,1)S(1)} %get-tuple-element.13.rth, bf16[768,384]{1,0:T(8,128)(2,1)S(1)} %get-tuple-element.14.rtl), custom_call_target="tpu_custom_call" | custom-call | tf_op jit(solution)/shard_map/finish/pallas_call | solution.py:461

commit v2 on v1

--- a/solution.py
+++ b/solution.py
@@ -97,10 +97,10 @@
 
 
 def kernel(
-    waves, waves_row, damp_row, circle, modes_in, modes_out, order, order_t, grid, plm,
+    waves, waves_all, damp_row, circle, modes_in, modes_out, order, order_t, grid, plm,
     gf, th, tl, rth, rtl,
     gh, gl, pf, ph, pw, s1, r1, s2, r2, x, e, acc, modes, damp,
-    circle_v, min_v, mout_v, order_v, order_tv, near_cos, near_sin, far,
+    circle_v, min_v, mout_v, order_v, order_tv, near_cos, near_sin, far, waves_row,
     load_sem, send1, recv1, send2, recv2,
 ):
     w = lax.axis_index("wave")
@@ -116,14 +116,16 @@
             ]
         )
     ]
+    row_copy = pltpu.make_async_copy(waves_all, waves_row.at[0], load_sem.at[7])
+    row_copy.start()
     small[0].start()
     for p in range(16):
         pltpu.make_async_copy(
-            grid.at[lax.rem(p - w + 16, 16)], gf.at[pl.ds(LT * p, LT)], load_sem.at[0]
+            grid.at[lax.rem(p - w + 16, 16)], gf.at[pl.ds(128 + LT * p, LT)], load_sem.at[0]
         ).start()
     for s in range(SLOTS):
         pltpu.make_async_copy(
-            grid.at[16], gf.at[pl.ds(16 * LT + LT * s, LT)], load_sem.at[0]
+            grid.at[16], gf.at[pl.ds(LT * s, LT)], load_sem.at[0]
         ).start()
 
     barrier = pltpu.get_barrier_semaphore()
@@ -141,6 +143,7 @@
     eye = lax.broadcasted_iota(jnp.int32, (slots, slots), 0) == lax.broadcasted_iota(
         jnp.int32, (slots, slots), 1
     )
+    row_copy.wait()
     column = jnp.sum(
         jnp.where(eye, waves_row[...].astype(f32), 0.0), axis=1, keepdims=True
     ).astype(jnp.int32)
@@ -155,28 +158,26 @@
     near_sin[...] = rows3[:, 128:256]
     far[...] = rows3[:, 256:384]
 
-    for s in range(SLOTS):
-
-        def table(i, carry):
-            mine = pl.ds(s + 96 * i, 32, SLOTS)
-            rows = pl.ds(pl.multiple_of(32 * i + 128 * s, 32), 32)
-            rows_sin = pl.ds(pl.multiple_of(32 * i + 128 * s + 384, 32), 32)
-            c1, n1, f = near_cos[mine, :], near_sin[mine, :], far[mine, :]
-            for a in range(LON // 128):
-                ca, sa = f[:, a : a + 1], f[:, 16 + a : 17 + a]
-                col = slice(128 * a, 128 * a + 128)
-                hi, lo = split(c1 * ca - n1 * sa)
-                th[rows, col] = hi
-                tl[rows, col] = lo
-                hi, lo = split(-(n1 * ca + c1 * sa))
-                th[rows_sin, col] = hi
-                tl[rows_sin, col] = lo
-            return carry
-
-        lax.fori_loop(0, 4, table, 0)
+    def make_table(c):
+        for s in range(SLOTS):
+
+            def table(i, carry):
+                mine = pl.ds(s + 96 * i, 32, SLOTS)
+                rows = pl.ds(pl.multiple_of(32 * i + 128 * s + 384 * c, 32), 32)
+                c1, n1, f = near_cos[mine, :], near_sin[mine, :], far[mine, :]
+                for a in range(LON // 128):
+                    ca, sa = f[:, a : a + 1], f[:, 16 + a : 17 + a]
+                    value = c1 * ca - n1 * sa if c == 0 else -(n1 * ca + c1 * sa)
+                    col = slice(128 * a, 128 * a + 128)
+                    th[rows, col], tl[rows, col] = split(value)
+                return carry
+
+            lax.fori_loop(0, 4, table, 0)
+
+    make_table(0)
 
     pltpu.make_async_copy(gf.at[pl.ds(0, 760)], gf.at[pl.ds(0, 760)], load_sem.at[0]).wait()
-    gf[760:768, :] = jnp.zeros((8, LON), f32)
+    gf[120:128, :] = jnp.zeros((8, LON), f32)
 
     def split_grid(i, carry):
         rows = pl.ds(pl.multiple_of(32 * i, 32), 32)
@@ -187,68 +188,61 @@
 
     lane128 = lanes(128)
 
-    def forward_dft(c):
-        def step(n, carry):
-            cols = pl.ds(pl.multiple_of(256 * n, 256), 256)
-            part = slice(384 * c, 384 * c + 384)
-            y = dot3(th[part, :], tl[part, :], gh[cols, :], gl[cols, :], NT)
-            for h in range(2):
-                yh = y[:, 128 * h : 128 * h + 128]
-
-                def main():
-                    for s in range(SLOTS):
-                        start = HALF * c + MAIN * s + 2 * n + h
-                        s1[pl.ds(start, DEVS, ROWS), :] = yh[128 * s : 128 * s + 128]
-
-                if h == 0:
-                    main()
-                else:
-                    pl.when(n < 2)(main)
-
-                    @pl.when(n == 2)
-                    def _():
-                        last = jnp.where(
-                            lane128 < LT,
-                            yh[0:128],
-                            jnp.where(lane128 < 2 * LT, yh[128:256], yh[256:384]),
-                        )
-                        s1[pl.ds(HALF * c + ROWS - 1, DEVS, ROWS), :] = last
-
-            return carry
-
-        lax.fori_loop(0, 3, step, 0)
-
-    def block(c, d):
-        return pl.ds(pl.multiple_of((c * DEVS + d) * ROWS, ROWS), ROWS)
-
-    def send(c, src, dst, send_sem, recv_sem):
-        pltpu.make_async_copy(src.at[block(c, me)], dst.at[block(c, me)], recv_sem.at[c]).start()
+    def forward_dft(c, n):
+        cols = slice(256 * n, 256 * n + 256)
+        part = slice(384 * c, 384 * c + 384)
+        y = dot3(th[part, :], tl[part, :], gh[cols, :], gl[cols, :], NT)
+        for h in range(2):
+            yh = y[:, 128 * h : 128 * h + 128]
+            t = 2 * n + h - 1
+            if t >= 0:
+                for s in range(SLOTS):
+                    start = HALF * c + 1 + 3 * t + s
+                    s1[pl.ds(start, DEVS, ROWS), :] = yh[128 * s : 128 * s + 128]
+            else:
+                last = jnp.where(
+                    lane128 < LT,
+                    yh[0:128],
+                    jnp.where(lane128 < 2 * LT, yh[128:256], yh[256:384]),
+                )
+                s1[pl.ds(HALF * c, DEVS, ROWS), :] = last
+
+    def send(c, first, rows, index, src, dst, send_sem, recv_sem):
+        def block(d):
+            return pl.ds(pl.multiple_of((c * DEVS + d) * ROWS + first, rows), rows)
+
+        pltpu.make_async_copy(src.at[block(me)], dst.at[block(me)], recv_sem.at[index]).start()
 
         def go(to_wave, to_lev):
             pltpu.make_async_remote_copy(
-                src_ref=src.at[block(c, to_wave * LEVS + to_lev)],
-                dst_ref=dst.at[block(c, me)],
-                send_sem=send_sem.at[c],
-                recv_sem=recv_sem.at[c],
+                src_ref=src.at[block(to_wave * LEVS + to_lev)],
+                dst_ref=dst.at[block(me)],
+                send_sem=send_sem.at[index],
+                recv_sem=recv_sem.at[index],
                 device_id=(to_wave, to_lev),
                 device_id_type=MESH,
             ).start()
 
         each_peer(go)
 
-    def arrive(c, dst, recv_sem):
-        half = dst.at[pl.ds(HALF * c, HALF)]
-        pltpu.make_async_copy(half, half, recv_sem.at[c]).wait()
-
-    def sent(c, src, send_sem):
-        part = src.at[pl.ds(0, HALF - ROWS)]
-        pltpu.make_async_copy(part, part, send_sem.at[c]).wait()
-
-    forward_dft(0)
+    def arrive(rows, index, dst, recv_sem):
+        part = dst.at[pl.ds(0, DEVS * rows)]
+        pltpu.make_async_copy(part, part, recv_sem.at[index]).wait()
+
+    def sent(rows, index, src, send_sem):
+        part = src.at[pl.ds(0, (DEVS - 1) * rows)]
+        pltpu.make_async_copy(part, part, send_sem.at[index]).wait()
+
+    forward_dft(0, 0)
+    forward_dft(0, 1)
     pl.semaphore_wait(barrier, DEVS - 1)
-    send(0, s1, r1, send1, recv1)
-    forward_dft(1)
-    send(1, s1, r1, send1, recv1)
+    send(0, 0, 8, 0, s1, r1, send1, recv1)
+    forward_dft(0, 2)
+    send(0, 8, 8, 1, s1, r1, send1, recv1)
+    make_table(1)
+    for n in range(3):
+        forward_dft(1, n)
+    send(1, 0, 16, 2, s1, r1, send1, recv1)
 
     pltpu.make_async_copy(pf, pf, load_sem.at[1]).wait()
 
@@ -277,17 +271,17 @@
         acc[...] = jnp.zeros((WAVES * 8, 128), f32)
 
         def slot(s, carry):
-            base = HALF * c + MAIN * s
+            base = HALF * c + 1 + s
             for k in range(16):
                 tiles = [
-                    pick(t, lambda p: r1[pl.ds(base + ((p - k) % 16) * 128 + t, 8, ROWS), :])
+                    pick(t, lambda p: r1[pl.ds(base + ((p - k) % 16) * 128 + 3 * t, 8, ROWS), :])
                     for t in range(MAIN)
                 ]
                 for t, value in enumerate(ring(tiles, LT * k)):
                     x[8 * k : 8 * k + 8, 128 * t : 128 * t + 128] = value
             tiles = [None] * MAIN
             for q in range(WAVES):
-                own = r1[pl.ds(HALF * c + q * 128 + ROWS - 1, 8, ROWS), :]
+                own = r1[pl.ds(HALF * c + q * 128, 8, ROWS), :]
                 own = pltpu.roll(own, lax.rem(LT * q - LT * s + 768, 128), 1)
                 t, off = divmod(LT * q, 128)
                 tiles[t] = own if off == 0 else jnp.where(lane8 < off, tiles[t], own)
@@ -320,7 +314,7 @@
                         k = (p - q) % 16
                         return e[8 * k : 8 * k + 8, 128 * t : 128 * t + 128]
 
-                    s2[pl.ds(base + q * 128 + t, 8, ROWS), :] = pick(t, get)
+                    s2[pl.ds(base + q * 128 + 3 * t, 8, ROWS), :] = pick(t, get)
                 t, off = divmod(LT * q, 128)
                 own = x[128:136, 128 * t : 128 * t + 128]
                 if off + LT > 128:
@@ -332,28 +326,30 @@
             return carry
 
         lax.fori_loop(0, SLOTS, slot, 0)
-        s2[pl.ds(HALF * c + ROWS - 1, DEVS, ROWS), :] = acc[...]
-
-    for c in range(2):
-        arrive(c, r1, recv1)
-        middle(c)
-        send(c, s2, r2, send2, recv2)
-
-    def transpose(c):
-        for s in range(SLOTS):
-            for t in range(MAIN):
-                tile = r2[pl.ds(HALF * c + MAIN * s + t, DEVS, ROWS), :]
-                hi, lo = split(tile.T)
-                rth[128 * t : 128 * t + 128, 128 * s : 128 * s + 128] = hi
-                rtl[128 * t : 128 * t + 128, 128 * s : 128 * s + 128] = lo
-            tile = r2[pl.ds(HALF * c + ROWS - 1, DEVS, ROWS), :]
-            inside = (lane128 >= LT * s) & (lane128 < LT * s + LT)
-            hi, lo = split(jnp.where(inside, tile, 0.0).T)
-            rth[128 * MAIN :, 128 * s : 128 * s + 128] = hi
-            rtl[128 * MAIN :, 128 * s : 128 * s + 128] = lo
-
-    arrive(0, r2, recv2)
-    transpose(0)
+        s2[pl.ds(HALF * c, DEVS, ROWS), :] = acc[...]
+
+    arrive(8, 0, r1, recv1)
+    arrive(8, 1, r1, recv1)
+    middle(0)
+    send(0, 0, 16, 2, s2, r2, send2, recv2)
+    arrive(16, 2, r1, recv1)
+    middle(1)
+    send(1, 0, 8, 0, s2, r2, send2, recv2)
+    send(1, 8, 8, 1, s2, r2, send2, recv2)
+
+    def transpose(c, tiles):
+        for t in tiles:
+            for s in range(SLOTS):
+                if t < 0:
+                    tile = r2[pl.ds(HALF * c, DEVS, ROWS), :]
+                    tile = jnp.where((lane128 >= LT * s) & (lane128 < LT * s + LT), tile, 0.0)
+                else:
+                    tile = r2[pl.ds(HALF * c + 1 + 3 * t + s, DEVS, ROWS), :]
+                where = (slice(128 * t + 128, 128 * t + 256), slice(128 * s, 128 * s + 128))
+                rth[where], rtl[where] = split(tile.T)
+
+    arrive(16, 2, r2, recv2)
+    transpose(0, range(-1, MAIN))
 
     def adjoint(n, carry):
         cols = pl.ds(pl.multiple_of(256 * n, 256), 256)
@@ -361,26 +357,52 @@
         return carry
 
     lax.fori_loop(0, LON // 256, adjoint, 0)
-    for c in range(2):
-        sent(c, s1, send1)
-        sent(c, s2, send2)
-    arrive(1, r2, recv2)
-    transpose(1)
-
-
-def finish(gf, th, tl, rth, rtl, out, block, sem):
+    for index, rows in ((0, 8), (1, 8), (2, 16)):
+        sent(rows, index, s1, send1)
+    sent(16, 2, s2, send2)
+    arrive(8, 0, r2, recv2)
+    transpose(1, range(-1, 2))
+
+    def adjoint_rest(n, carry):
+        cols = pl.ds(pl.multiple_of(256 * n, 256), 256)
+        gf[0:384, cols] += dot3(
+            rth[0:384, :], rtl[0:384, :], th[384:768, cols], tl[384:768, cols], NN
+        )
+        return carry
+
+    lax.fori_loop(0, LON // 256, adjoint_rest, 0)
+    gf[0:40, :] = gf[0:40, :] + gf[40:80, :] + gf[80:120, :]
+    sent(8, 0, s2, send2)
+    arrive(8, 1, r2, recv2)
+    transpose(1, range(2, MAIN))
+    sent(8, 1, s2, send2)
+
+
+def finish(gf, th, tl, rth, rtl, out, rest, sem):
     w = lax.axis_index("wave")
     copies = []
-    for n in range(LON // 256):
-        cols = slice(256 * n, 256 * n + 256)
-        y = gf[:, cols] + dot3(rth[...], rtl[...], th[384:768, cols], tl[384:768, cols], NN)
-        for p in range(16):
-            level = lax.rem(p - w + 16, 16)
-            block[n, pl.ds(pl.multiple_of(LT * level, 8), LT), :] = y[LT * p : LT * p + LT]
-        block[n, 640:680, :] = y[640:680] + y[680:720] + y[720:760]
-        copy = pltpu.make_async_copy(block.at[n], out.at[:, cols], sem.at[n])
+
+    def write(src, dst, index):
+        copy = pltpu.make_async_copy(src, dst, sem.at[index])
         copy.start()
         copies.append(copy)
+
+    write(gf.at[pl.ds(0, LT)], out.at[16], 0)
+    for p in range(6):
+        write(gf.at[pl.ds(128 + LT * p, LT)], out.at[lax.rem(p - w + 16, 16)], 1 + p)
+    rest[0:16, :] = gf[368:384, :]
+    index = 7
+    for cols in (slice(0, 512), slice(512, 1024), slice(1024, 1280)):
+        rest[16:400, cols] = gf[384:768, cols] + dot3(
+            rth[384:768, :], rtl[384:768, :], th[384:768, cols], tl[384:768, cols], NN
+        )
+        for p in range(6, 16):
+            write(
+                rest.at[pl.ds(LT * (p - 6), LT), cols],
+                out.at[lax.rem(p - w + 16, 16), :, cols],
+                index,
+            )
+            index += 1
     for copy in copies:
         copy.wait()
 
@@ -418,7 +440,7 @@
             pltpu.VMEM((768, 384), bf16),
             pltpu.VMEM((768, 384), bf16),
         ],
-        in_specs=[pl.BlockSpec(memory_space=pltpu.SMEM)] + [vmem] * 2 + [hbm] * 7,
+        in_specs=[pl.BlockSpec(memory_space=pltpu.SMEM), hbm, vmem] + [hbm] * 7,
         out_specs=[vmem] * 5,
         scratch_shapes=[
             pltpu.VMEM((768, LON), bf16),
@@ -443,29 +465,30 @@
             pltpu.VMEM((DEVS * SLOTS, 128), f32),
             pltpu.VMEM((DEVS * SLOTS, 128), f32),
             pltpu.VMEM((DEVS * SLOTS, 128), f32),
-            dma((7,)),
-            dma((2,)),
-            dma((2,)),
-            dma((2,)),
-            dma((2,)),
+            pltpu.VMEM((1, DEVS * SLOTS), jnp.int32),
+            dma((8,)),
+            dma((3,)),
+            dma((3,)),
+            dma((3,)),
+            dma((3,)),
         ],
         compiler_params=pltpu.CompilerParams(
             collective_id=0, has_side_effects=True, vmem_limit_bytes=48 << 20
         ),
         name="spectral_step",
     )(
-        wavenumbers, wavenumbers.reshape(1, -1), damping.reshape(1, -1), jnp.asarray(circle_table()),
+        wavenumbers, wavenumbers, damping.reshape(1, -1), jnp.asarray(circle_table()),
         modes_in, modes_out, jnp.asarray(order), jnp.asarray(order.T.copy()),
         grid_in.reshape(LV, LT, LON), legendre,
     )
     result = pl.pallas_call(
         finish,
-        out_shape=jax.ShapeDtypeStruct((LV * LT, LON), f32),
+        out_shape=jax.ShapeDtypeStruct((LV, LT, LON), f32),
         in_specs=[vmem] * 5,
         out_specs=hbm,
         scratch_shapes=[
-            pltpu.VMEM((LON // 256, LV * LT, 256), f32),
-            dma((LON // 256,)),
+            pltpu.VMEM((400, LON), f32),
+            dma((37,)),
         ],
         compiler_params=pltpu.CompilerParams(vmem_limit_bytes=40 << 20),
         name="finish",

time: 70.3 us -> 67 us (0.953)
  Pallas kernels: 68.9 us -> 66.7 us
  local copies, waits for them, and re-layouts: 1.24 us -> 0 us
    pallas_call x1, Pallas kernels: 4.18 us -> 2.92 us  [local(): pl.pallas_call(finish, out_shape=jax.ShapeDtypeStruct((LV, LT, LON), f32)...]
    reshape x1 -> x0, local copies, waits for them, and re-layouts: 1.24 us -> none  [local(): wavenumbers.reshape(1, -1)]
    pallas_call x1, Pallas kernels: 64.7 us -> 63.7 us  [local(): pl.pallas_call(kernel, out_shape=[pltpu.VMEM((768, LON), f32), pltpu.VMEM...]
where the time goes in v2:
time: 67 us; the launch traced here: 66.8 us
  Pallas kernels  66.7 us (100%)
    pallas_call x1, Pallas kernels, local(): pl.pallas_call(kernel, out_shape=[pltpu.VMEM((768, LON), f32), pltpu.VMEM...  63.7 us
    pallas_call x1, Pallas kernels, local(): pl.pallas_call(finish, out_shape=jax.ShapeDtypeStruct((LV, LT, LON), f32)...  2.92 us

profile of v2, /device:TPU:1, one launch (start us, length us, event | category | flops | bytes accessed | tf_op | source)
XLA Modules:
  0.0 66.8 jit_solution(1356080628703817191)
XLA Ops:
  0.0 63.7 %spectral_step.1 = (f32[768,1280]{1,0:T(8,128)S(1)}, bf16[768,1280]{1,0:T(8,128)(2,1)S(1)}, bf16[768,1280]{1,0:T(8,128)(2,1)S(1)}, bf16[768,384]{1,0:T(8,128)(2,1)S(1)}, bf16[768,384]{1,0:T(8,128)(2,1)S(1)}) custom-call(s32[384]{0:T(512)} %waves_all.1, s32[384]{0:T(512)} %waves_all.1, f32[1,136]{1,0:T(1,128)} %bitcast.4, f32[384,384]{1,0:T(8,128)} %constant.6.clone.circle, ...), custom_call_target="tpu_custom_call" | custom-call | tf_op jit(solution)/shard_map/spectral_step/pallas_call | solution.py:434
  63.7 2.9 %finish.1 = f32[17,40,1280]{2,1,0:T(8,128)} custom-call(f32[768,1280]{1,0:T(8,128)S(1)} %get-tuple-element.10.gf, bf16[768,1280]{1,0:T(8,128)(2,1)S(1)} %get-tuple-element.11.th, bf16[768,1280]{1,0:T(8,128)(2,1)S(1)} %get-tuple-element.12.tl, bf16[768,384]{1,0:T(8,128)(2,1)S(1)} %get-tuple-element.13.rth, bf16[768,384]{1,0:T(8,128)(2,1)S(1)} %get-tuple-element.14.rtl), custom_call_target="tpu_custom_call" | custom-call | tf_op jit(solution)/shard_map/finish/pallas_call | solution.py:484

commit v3 on v2

--- a/solution.py
+++ b/solution.py
@@ -43,7 +43,13 @@
 
 
 def dot3(ah, al, bh, bl, dims):
-    return dot(ah, bh, dims) + dot(al, bh, dims) + dot(ah, bl, dims)
+    rows = ah.shape[0]
+    both = dot(jnp.concatenate([ah, al], 0), bh, dims)
+    return both[:rows] + both[rows:] + dot(ah, bl, dims)
+
+
+def dot3_deep(ah, al, bh, bl):
+    return dot(jnp.concatenate([ah, al, ah], 1), jnp.concatenate([bh, bh, bl], 0), NN)
 
 
 def lanes(rows):
@@ -119,25 +125,29 @@
     row_copy = pltpu.make_async_copy(waves_all, waves_row.at[0], load_sem.at[7])
     row_copy.start()
     small[0].start()
-    for p in range(16):
-        pltpu.make_async_copy(
-            grid.at[lax.rem(p - w + 16, 16)], gf.at[pl.ds(128 + LT * p, LT)], load_sem.at[0]
-        ).start()
     for s in range(SLOTS):
         pltpu.make_async_copy(
             grid.at[16], gf.at[pl.ds(LT * s, LT)], load_sem.at[0]
         ).start()
 
+    def load_level(p):
+        pltpu.make_async_copy(
+            grid.at[lax.rem(p - w + 16, 16)],
+            gf.at[pl.ds(128 + LT * p, LT)],
+            load_sem.at[0 if p < 4 else 7 + (p + 2) // 6],
+        ).start()
+
+    for p in range(4):
+        load_level(p)
+
     barrier = pltpu.get_barrier_semaphore()
 
     def greet(to_wave, to_lev):
         pl.semaphore_signal(barrier, inc=1, device_id=(to_wave, to_lev), device_id_type=MESH)
 
     each_peer(greet)
-    for copy in small[1:]:
-        copy.start()
-    for s in range(SLOTS):
-        pltpu.make_async_copy(plm.at[s], pf.at[pl.ds(LAT * s, LAT)], load_sem.at[1]).start()
+    for p in range(4, 16):
+        load_level(p)
 
     slots = DEVS * SLOTS
     eye = lax.broadcasted_iota(jnp.int32, (slots, slots), 0) == lax.broadcasted_iota(
@@ -149,67 +159,64 @@
     ).astype(jnp.int32)
     chosen = (lax.broadcasted_iota(jnp.int32, (slots, slots), 1) == column).astype(bf16)
     small[0].wait()
-    rest = circle_v[...]
-    top, _ = split(rest)
-    rest = rest - top.astype(f32)
-    mid, low = split(rest)
-    rows3 = dot(chosen, top, NN) + dot(chosen, mid, NN) + dot(chosen, low, NN)
+    top, rest = split(circle_v[...])
+    rows3 = dot(chosen, top, NN) + dot(chosen, rest, NN)
     near_cos[...] = rows3[:, 0:128]
     near_sin[...] = rows3[:, 128:256]
     far[...] = rows3[:, 256:384]
 
     def make_table(c):
-        for s in range(SLOTS):
-
-            def table(i, carry):
-                mine = pl.ds(s + 96 * i, 32, SLOTS)
-                rows = pl.ds(pl.multiple_of(32 * i + 128 * s + 384 * c, 32), 32)
-                c1, n1, f = near_cos[mine, :], near_sin[mine, :], far[mine, :]
-                for a in range(LON // 128):
-                    ca, sa = f[:, a : a + 1], f[:, 16 + a : 17 + a]
-                    value = c1 * ca - n1 * sa if c == 0 else -(n1 * ca + c1 * sa)
-                    col = slice(128 * a, 128 * a + 128)
-                    th[rows, col], tl[rows, col] = split(value)
-                return carry
-
-            lax.fori_loop(0, 4, table, 0)
-
-    make_table(0)
-
-    pltpu.make_async_copy(gf.at[pl.ds(0, 760)], gf.at[pl.ds(0, 760)], load_sem.at[0]).wait()
-    gf[120:128, :] = jnp.zeros((8, LON), f32)
+        def table(s, carry):
+            mine = pl.ds(s, DEVS, SLOTS)
+            rows = pl.ds(pl.multiple_of(384 * c + DEVS * s, DEVS), DEVS)
+            cosine, sine, f = near_cos[mine, :], near_sin[mine, :], far[mine, :]
+            first = jnp.where(c == 0, cosine, -sine)
+            second = jnp.where(c == 0, sine, cosine)
+            for a in range(LON // 128):
+                ca, sa = f[:, a : a + 1], f[:, 16 + a : 17 + a]
+                col = slice(128 * a, 128 * a + 128)
+                th[rows, col], tl[rows, col] = split(first * ca - second * sa)
+            return carry
+
+        lax.fori_loop(0, SLOTS, table, 0)
+
+    def loaded(rows, index):
+        part = gf.at[pl.ds(0, rows)]
+        pltpu.make_async_copy(part, part, load_sem.at[index]).wait()
 
     def split_grid(i, carry):
         rows = pl.ds(pl.multiple_of(32 * i, 32), 32)
         gh[rows, :], gl[rows, :] = split(gf[rows, :])
         return carry
 
-    lax.fori_loop(0, 24, split_grid, 0)
-
     lane128 = lanes(128)
 
     def forward_dft(c, n):
-        cols = slice(256 * n, 256 * n + 256)
-        part = slice(384 * c, 384 * c + 384)
+        cols = pl.ds(pl.multiple_of(256 * n, 256), 256)
+        part = pl.ds(pl.multiple_of(384 * c, 128), 384)
         y = dot3(th[part, :], tl[part, :], gh[cols, :], gl[cols, :], NT)
-        for h in range(2):
-            yh = y[:, 128 * h : 128 * h + 128]
-            t = 2 * n + h - 1
-            if t >= 0:
-                for s in range(SLOTS):
-                    start = HALF * c + 1 + 3 * t + s
-                    s1[pl.ds(start, DEVS, ROWS), :] = yh[128 * s : 128 * s + 128]
-            else:
-                last = jnp.where(
-                    lane128 < LT,
-                    yh[0:128],
-                    jnp.where(lane128 < 2 * LT, yh[128:256], yh[256:384]),
-                )
-                s1[pl.ds(HALF * c, DEVS, ROWS), :] = last
-
-    def send(c, first, rows, index, src, dst, send_sem, recv_sem):
+        y0, y1 = y[:, 0:128], y[:, 128:256]
+
+        @pl.when(n == 0)
+        def _():
+            last = jnp.where(
+                lane128 < LT, y0[0:128], jnp.where(lane128 < 2 * LT, y0[128:256], y0[256:384])
+            )
+            s1[pl.ds(HALF * c, DEVS, ROWS), :] = last
+
+        @pl.when(n > 0)
+        def _():
+            for s in range(SLOTS):
+                s1[pl.ds(HALF * c + 6 * n - 2 + s, DEVS, ROWS), :] = y0[128 * s : 128 * s + 128]
+
+        for s in range(SLOTS):
+            s1[pl.ds(HALF * c + 6 * n + 1 + s, DEVS, ROWS), :] = y1[128 * s : 128 * s + 128]
+
+    def send(c, h, src, dst, send_sem, recv_sem):
+        index = 2 * c + h
+
         def block(d):
-            return pl.ds(pl.multiple_of((c * DEVS + d) * ROWS + first, rows), rows)
+            return pl.ds(pl.multiple_of((c * DEVS + d) * ROWS + 8 * h, 8), 8)
 
         pltpu.make_async_copy(src.at[block(me)], dst.at[block(me)], recv_sem.at[index]).start()
 
@@ -225,24 +232,56 @@
 
         each_peer(go)
 
-    def arrive(rows, index, dst, recv_sem):
-        part = dst.at[pl.ds(0, DEVS * rows)]
+    def arrive(index, dst, recv_sem):
+        part = dst.at[pl.ds(0, DEVS * 8)]
         pltpu.make_async_copy(part, part, recv_sem.at[index]).wait()
 
-    def sent(rows, index, src, send_sem):
-        part = src.at[pl.ds(0, (DEVS - 1) * rows)]
+    def sent(index, src, send_sem):
+        part = src.at[pl.ds(0, (DEVS - 1) * 8)]
         pltpu.make_async_copy(part, part, send_sem.at[index]).wait()
 
-    forward_dft(0, 0)
-    forward_dft(0, 1)
-    pl.semaphore_wait(barrier, DEVS - 1)
-    send(0, 0, 8, 0, s1, r1, send1, recv1)
-    forward_dft(0, 2)
-    send(0, 8, 8, 1, s1, r1, send1, recv1)
-    make_table(1)
-    for n in range(3):
-        forward_dft(1, n)
-    send(1, 0, 16, 2, s1, r1, send1, recv1)
+    def forward(i, carry):
+        c, n = i // 3, lax.rem(i, 3)
+
+        @pl.when(n == 0)
+        def _():
+            make_table(c)
+
+        @pl.when(i == 0)
+        def _():
+            loaded(7 * LT, 0)
+            gf[120:128, :] = jnp.zeros((8, LON), f32)
+
+        @pl.when((i == 1) | (i == 2))
+        def _():
+            loaded(6 * LT, 7 + i)
+
+        @pl.when(i == 2)
+        def _():
+            for copy in small[1:]:
+                copy.start()
+            for s in range(SLOTS):
+                pltpu.make_async_copy(
+                    plm.at[s], pf.at[pl.ds(LAT * s, LAT)], load_sem.at[1]
+                ).start()
+
+        @pl.when(c == 0)
+        def _():
+            lax.fori_loop(8 * n, 8 * n + 8, split_grid, 0)
+
+        forward_dft(c, n)
+
+        @pl.when(i == 1)
+        def _():
+            pl.semaphore_wait(barrier, DEVS - 1)
+
+        @pl.when(n > 0)
+        def _():
+            send(c, n - 1, s1, r1, send1, recv1)
+
+        return carry
+
+    lax.fori_loop(0, 6, forward, 0)
 
     pltpu.make_async_copy(pf, pf, load_sem.at[1]).wait()
 
@@ -267,7 +306,9 @@
     x[LEVELS:PAD, :] = jnp.zeros((PAD - LEVELS, LAT), f32)
     lane8 = lanes(8)
 
-    def middle(c):
+    def middle(c, outer):
+        arrive(2 * c, r1, recv1)
+        arrive(2 * c + 1, r1, recv1)
         acc[...] = jnp.zeros((WAVES * 8, 128), f32)
 
         def slot(s, carry):
@@ -328,54 +369,56 @@
         lax.fori_loop(0, SLOTS, slot, 0)
         s2[pl.ds(HALF * c, DEVS, ROWS), :] = acc[...]
 
-    arrive(8, 0, r1, recv1)
-    arrive(8, 1, r1, recv1)
-    middle(0)
-    send(0, 0, 16, 2, s2, r2, send2, recv2)
-    arrive(16, 2, r1, recv1)
-    middle(1)
-    send(1, 0, 8, 0, s2, r2, send2, recv2)
-    send(1, 8, 8, 1, s2, r2, send2, recv2)
-
-    def transpose(c, tiles):
-        for t in tiles:
+
+        def out_half(h, carry):
+            send(c, h, s2, r2, send2, recv2)
+            return carry
+
+        lax.fori_loop(0, 2, out_half, 0)
+        return outer
+
+    lax.fori_loop(0, 2, middle, 0)
+
+    def returned(j, carry):
+        c, h = j // 2, lax.rem(j, 2)
+        rows = pl.ds(pl.multiple_of(384 * h, 128), 384)
+        part = pl.ds(pl.multiple_of(384 * c, 128), 384)
+        arrive(j, r2, recv2)
+
+        for i in range(3):
+            u = 3 * h + i
+            rows_u = pl.ds(pl.multiple_of(128 * u, 128), 128)
             for s in range(SLOTS):
-                if t < 0:
-                    tile = r2[pl.ds(HALF * c, DEVS, ROWS), :]
-                    tile = jnp.where((lane128 >= LT * s) & (lane128 < LT * s + LT), tile, 0.0)
-                else:
-                    tile = r2[pl.ds(HALF * c + 1 + 3 * t + s, DEVS, ROWS), :]
-                where = (slice(128 * t + 128, 128 * t + 256), slice(128 * s, 128 * s + 128))
-                rth[where], rtl[where] = split(tile.T)
-
-    arrive(16, 2, r2, recv2)
-    transpose(0, range(-1, MAIN))
-
-    def adjoint(n, carry):
-        cols = pl.ds(pl.multiple_of(256 * n, 256), 256)
-        gf[:, cols] = dot3(rth[...], rtl[...], th[0:384, cols], tl[0:384, cols], NN)
+                start = jnp.where(u == 0, 0, 3 * u - 2 + s)
+                tile = r2[pl.ds(HALF * c + start, DEVS, ROWS), :]
+                if i == 0:
+                    inside = (lane128 >= LT * s) & (lane128 < LT * s + LT)
+                    tile = jnp.where(inside | (u > 0), tile, 0.0)
+                cols_s = slice(128 * s, 128 * s + 128)
+                rth[rows_u, cols_s], rtl[rows_u, cols_s] = split(tile.T)
+
+        @pl.when(j < 3)
+        def _():
+            def adjoint(n, inner):
+                cols = pl.ds(pl.multiple_of(256 * n, 256), 256)
+                y = dot3_deep(rth[rows, :], rtl[rows, :], th[part, cols], tl[part, cols])
+                gf[rows, cols] = jnp.where(c == 0, y, gf[rows, cols] + y)
+                return inner
+
+            lax.fori_loop(0, LON // 256, adjoint, 0)
+
+        @pl.when(j == 2)
+        def _():
+            gf[0:40, :] = gf[0:40, :] + gf[40:80, :] + gf[80:120, :]
+            for index in range(4):
+                sent(index, s1, send1)
+            for index in range(3):
+                sent(index, s2, send2)
+
         return carry
 
-    lax.fori_loop(0, LON // 256, adjoint, 0)
-    for index, rows in ((0, 8), (1, 8), (2, 16)):
-        sent(rows, index, s1, send1)
-    sent(16, 2, s2, send2)
-    arrive(8, 0, r2, recv2)
-    transpose(1, range(-1, 2))
-
-    def adjoint_rest(n, carry):
-        cols = pl.ds(pl.multiple_of(256 * n, 256), 256)
-        gf[0:384, cols] += dot3(
-            rth[0:384, :], rtl[0:384, :], th[384:768, cols], tl[384:768, cols], NN
-        )
-        return carry
-
-    lax.fori_loop(0, LON // 256, adjoint_rest, 0)
-    gf[0:40, :] = gf[0:40, :] + gf[40:80, :] + gf[80:120, :]
-    sent(8, 0, s2, send2)
-    arrive(8, 1, r2, recv2)
-    transpose(1, range(2, MAIN))
-    sent(8, 1, s2, send2)
+    lax.fori_loop(0, 4, returned, 0)
+    sent(3, s2, send2)
 
 
 def finish(gf, th, tl, rth, rtl, out, rest, sem):
@@ -391,18 +434,22 @@
     for p in range(6):
         write(gf.at[pl.ds(128 + LT * p, LT)], out.at[lax.rem(p - w + 16, 16)], 1 + p)
     rest[0:16, :] = gf[368:384, :]
-    index = 7
-    for cols in (slice(0, 512), slice(512, 1024), slice(1024, 1280)):
-        rest[16:400, cols] = gf[384:768, cols] + dot3(
-            rth[384:768, :], rtl[384:768, :], th[384:768, cols], tl[384:768, cols], NN
+
+    def step(n, carry):
+        cols = pl.ds(pl.multiple_of(256 * n, 256), 256)
+        rest[16:400, cols] = gf[384:768, cols] + dot3_deep(
+            rth[384:768, :], rtl[384:768, :], th[384:768, cols], tl[384:768, cols]
         )
         for p in range(6, 16):
-            write(
+            pltpu.make_async_copy(
                 rest.at[pl.ds(LT * (p - 6), LT), cols],
                 out.at[lax.rem(p - w + 16, 16), :, cols],
-                index,
-            )
-            index += 1
+                sem.at[7],
+            ).start()
+        return carry
+
+    lax.fori_loop(0, LON // 256, step, 0)
+    pltpu.make_async_copy(rest, rest, sem.at[7]).wait()
     for copy in copies:
         copy.wait()
 
@@ -466,11 +513,11 @@
             pltpu.VMEM((DEVS * SLOTS, 128), f32),
             pltpu.VMEM((DEVS * SLOTS, 128), f32),
             pltpu.VMEM((1, DEVS * SLOTS), jnp.int32),
-            dma((8,)),
-            dma((3,)),
-            dma((3,)),
-            dma((3,)),
-            dma((3,)),
+            dma((10,)),
+            dma((4,)),
+            dma((4,)),
+            dma((4,)),
+            dma((4,)),
         ],
         compiler_params=pltpu.CompilerParams(
             collective_id=0, has_side_effects=True, vmem_limit_bytes=48 << 20
@@ -488,7 +535,7 @@
         out_specs=hbm,
         scratch_shapes=[
             pltpu.VMEM((400, LON), f32),
-            dma((37,)),
+            dma((8,)),
         ],
         compiler_params=pltpu.CompilerParams(vmem_limit_bytes=40 << 20),
         name="finish",

time: 67 us -> 66 us (0.985)
  Pallas kernels: 66.7 us -> 65.9 us
    pallas_call x1, Pallas kernels: 63.7 us -> 62.8 us  [local(): pl.pallas_call(kernel, out_shape=[pltpu.VMEM((768, LON), f32), pltpu.VMEM...]
where the time goes in v3:
time: 66 us; the launch traced here: 65.9 us
  Pallas kernels  65.9 us (100%)
    pallas_call x1, Pallas kernels, local(): pl.pallas_call(kernel, out_shape=[pltpu.VMEM((768, LON), f32), pltpu.VMEM...  62.8 us
    pallas_call x1, Pallas kernels, local(): pl.pallas_call(finish, out_shape=jax.ShapeDtypeStruct((LV, LT, LON), f32)...  3.06 us

profile of v3, /device:TPU:1, one launch (start us, length us, event | category | flops | bytes accessed | tf_op | source)
XLA Modules:
  0.0 65.9 jit_solution(3874115734848766982)
XLA Ops:
  0.0 62.8 %spectral_step.1 = (f32[768,1280]{1,0:T(8,128)S(1)}, bf16[768,1280]{1,0:T(8,128)(2,1)S(1)}, bf16[768,1280]{1,0:T(8,128)(2,1)S(1)}, bf16[768,384]{1,0:T(8,128)(2,1)S(1)}, bf16[768,384]{1,0:T(8,128)(2,1)S(1)}) custom-call(s32[384]{0:T(512)} %waves_all.1, s32[384]{0:T(512)} %waves_all.1, f32[1,136]{1,0:T(1,128)} %bitcast.4, f32[384,384]{1,0:T(8,128)} %constant.6.clone.circle, ...), custom_call_target="tpu_custom_call" | custom-call | tf_op jit(solution)/shard_map/spectral_step/pallas_call | solution.py:481
  62.9 3.1 %finish.1 = f32[17,40,1280]{2,1,0:T(8,128)} custom-call(f32[768,1280]{1,0:T(8,128)S(1)} %get-tuple-element.10.gf, bf16[768,1280]{1,0:T(8,128)(2,1)S(1)} %get-tuple-element.11.th, bf16[768,1280]{1,0:T(8,128)(2,1)S(1)} %get-tuple-element.12.tl, bf16[768,384]{1,0:T(8,128)(2,1)S(1)} %get-tuple-element.13.rth, bf16[768,384]{1,0:T(8,128)(2,1)S(1)} %get-tuple-element.14.rtl), custom_call_target="tpu_custom_call" | custom-call | tf_op jit(solution)/shard_map/finish/pallas_call | solution.py:531

commit v4 on v3

--- a/solution.py
+++ b/solution.py
@@ -102,27 +102,53 @@
         visit(wave_x[0] + 2 * lax.rem(z + j, 4) + lax.rem(core + j // 4, 2), lev_x[0] + lev_y[0])
 
 
+def far_first():
+    order = []
+    for i in range(1, DEVS):
+        a, b, d, core = i % 4, i // 4 % 4, i // 16 % 4, i // 64
+        order.append((a, (a + b) % 4, (b + d + 2 * a) % 4, core))
+    return sorted(order, key=lambda o: -sum(min(k, 4 - k) for k in o[:3]))
+
+
+def each_peer_far_first(visit):
+    x, y, z, core = coordinates()
+    xs = [lax.rem(x + a, 4) for a in range(4)]
+    wave_x = [8 * lax.rem(a, 2) for a in xs]
+    lev_x = [4 * (a // 2) for a in xs]
+    lev_y = [lax.rem(y + b, 4) for b in range(4)]
+    wave_z = [2 * lax.rem(z + d, 4) for d in range(4)]
+    wave_c = [core, 1 - core]
+    for a, b, d, other in far_first():
+        visit(wave_x[a] + wave_z[d] + wave_c[other], lev_x[a] + lev_y[b])
+
+
 def kernel(
-    waves, waves_all, damp_row, circle, modes_in, modes_out, order, order_t, grid, plm,
+    waves, damp_all, circle, modes_in, modes_out, order, order_t, grid, plm,
     gf, th, tl, rth, rtl,
     gh, gl, pf, ph, pw, s1, r1, s2, r2, x, e, acc, modes, damp,
-    circle_v, min_v, mout_v, order_v, order_tv, near_cos, near_sin, far, waves_row,
+    circle_v, min_v, mout_v, order_v, order_tv, near_cos, near_sin, far, waves_row, damp_row,
     load_sem, send1, recv1, send2, recv2,
 ):
     w = lax.axis_index("wave")
     v = lax.axis_index("lev")
     me = w * LEVS + v
 
+    barrier = pltpu.get_barrier_semaphore()
+
+    def greet(to_wave, to_lev):
+        pl.semaphore_signal(barrier, inc=1, device_id=(to_wave, to_lev), device_id_type=MESH)
+
+    each_peer(greet)
     small = [
-        pltpu.make_async_copy(a, b, load_sem.at[2 + i])
+        pltpu.make_async_copy(a, b, load_sem.at[2 + i if i < 5 else 10])
         for i, (a, b) in enumerate(
             [
                 (circle, circle_v), (modes_in, min_v), (modes_out, mout_v),
-                (order, order_v), (order_t, order_tv),
+                (order, order_v), (order_t, order_tv), (damp_all, damp_row),
             ]
         )
     ]
-    row_copy = pltpu.make_async_copy(waves_all, waves_row.at[0], load_sem.at[7])
+    row_copy = pltpu.make_async_copy(waves, waves_row.at[0], load_sem.at[7])
     row_copy.start()
     small[0].start()
     for s in range(SLOTS):
@@ -140,12 +166,6 @@
     for p in range(4):
         load_level(p)
 
-    barrier = pltpu.get_barrier_semaphore()
-
-    def greet(to_wave, to_lev):
-        pl.semaphore_signal(barrier, inc=1, device_id=(to_wave, to_lev), device_id_type=MESH)
-
-    each_peer(greet)
     for p in range(4, 16):
         load_level(p)
 
@@ -213,10 +233,12 @@
             s1[pl.ds(HALF * c + 6 * n + 1 + s, DEVS, ROWS), :] = y1[128 * s : 128 * s + 128]
 
     def send(c, h, src, dst, send_sem, recv_sem):
-        index = 2 * c + h
+        send_rows(each_peer, c, 8 * h, 8, 2 * c + h, src, dst, send_sem, recv_sem)
+
+    def send_rows(each, c, first, rows, index, src, dst, send_sem, recv_sem):
 
         def block(d):
-            return pl.ds(pl.multiple_of((c * DEVS + d) * ROWS + 8 * h, 8), 8)
+            return pl.ds(pl.multiple_of((c * DEVS + d) * ROWS + first, rows), rows)
 
         pltpu.make_async_copy(src.at[block(me)], dst.at[block(me)], recv_sem.at[index]).start()
 
@@ -230,14 +252,14 @@
                 device_id_type=MESH,
             ).start()
 
-        each_peer(go)
-
-    def arrive(index, dst, recv_sem):
-        part = dst.at[pl.ds(0, DEVS * 8)]
+        each(go)
+
+    def arrive(index, dst, recv_sem, rows=8):
+        part = dst.at[pl.ds(0, DEVS * rows)]
         pltpu.make_async_copy(part, part, recv_sem.at[index]).wait()
 
-    def sent(index, src, send_sem):
-        part = src.at[pl.ds(0, (DEVS - 1) * 8)]
+    def sent(index, src, send_sem, rows=8):
+        part = src.at[pl.ds(0, (DEVS - 1) * rows)]
         pltpu.make_async_copy(part, part, send_sem.at[index]).wait()
 
     def forward(i, carry):
@@ -271,11 +293,15 @@
 
         forward_dft(c, n)
 
-        @pl.when(i == 1)
+        @pl.when(i == 0)
         def _():
             pl.semaphore_wait(barrier, DEVS - 1)
 
-        @pl.when(n > 0)
+        @pl.when(i < 2)
+        def _():
+            send_rows(each_peer, 0, 4 * i, 4, 4 * i, s1, r1, send1, recv1)
+
+        @pl.when((n > 0) & (i != 1))
         def _():
             send(c, n - 1, s1, r1, send1, recv1)
 
@@ -307,7 +333,15 @@
     lane8 = lanes(8)
 
     def middle(c, outer):
-        arrive(2 * c, r1, recv1)
+        @pl.when(c == 0)
+        def _():
+            arrive(0, r1, recv1, 4)
+            arrive(4, r1, recv1, 4)
+
+        @pl.when(c == 1)
+        def _():
+            arrive(2, r1, recv1)
+
         arrive(2 * c + 1, r1, recv1)
         acc[...] = jnp.zeros((WAVES * 8, 128), f32)
 
@@ -334,7 +368,11 @@
             prow = pl.ds(pl.multiple_of(LAT * s, LAT), LAT)
             xh, xl = split(x[...])
             spec = dot3(xh, xl, ph[prow, :], pw[prow, :], NN)
-            degree = waves[SLOTS * me + s] + lax.broadcasted_iota(jnp.int32, (PAD, COEFF), 1)
+            here = lax.broadcasted_iota(jnp.int32, (1, slots), 1) == SLOTS * me + s
+            wave = jnp.sum(
+                jnp.where(here, waves_row[...].astype(f32), 0.0), axis=1, keepdims=True
+            ).astype(jnp.int32)
+            degree = wave + lax.broadcasted_iota(jnp.int32, (PAD, COEFF), 1)
             growth = (degree * (degree + 1)).astype(f32)
             factor = jnp.where(degree < COEFF, 1.0 / (1.0 + damp[...] * growth), 0.0)
             sh, sl = split(spec)
@@ -371,54 +409,77 @@
 
 
         def out_half(h, carry):
-            send(c, h, s2, r2, send2, recv2)
+            @pl.when((c == 0) | (h == 0))
+            def _():
+                send_rows(
+                    each_peer_far_first, c, 8 * h, 8, 2 * c + h, s2, r2, send2, recv2
+                )
+
+            @pl.when((c == 1) & (h > 0))
+            def _():
+                send_rows(
+                    each_peer_far_first, c, 4 + 4 * h, 4, 2 + h, s2, r2, send2, recv2
+                )
+
             return carry
 
-        lax.fori_loop(0, 2, out_half, 0)
+        lax.fori_loop(0, 2 + c, out_half, 0)
         return outer
 
     lax.fori_loop(0, 2, middle, 0)
+
+    def transpose(c, u, s):
+        start = jnp.where(u == 0, 0, 3 * u - 2 + s)
+        tile = r2[pl.ds(HALF * c + start, DEVS, ROWS), :]
+        inside = (lane128 >= LT * s) & (lane128 < LT * s + LT)
+        tile = jnp.where(inside | (u > 0), tile, 0.0)
+        rows_u = pl.ds(pl.multiple_of(128 * u, 128), 128)
+        cols_s = slice(128 * s, 128 * s + 128)
+        rth[rows_u, cols_s], rtl[rows_u, cols_s] = split(tile.T)
 
     def returned(j, carry):
         c, h = j // 2, lax.rem(j, 2)
         rows = pl.ds(pl.multiple_of(384 * h, 128), 384)
         part = pl.ds(pl.multiple_of(384 * c, 128), 384)
         arrive(j, r2, recv2)
-
         for i in range(3):
-            u = 3 * h + i
-            rows_u = pl.ds(pl.multiple_of(128 * u, 128), 128)
             for s in range(SLOTS):
-                start = jnp.where(u == 0, 0, 3 * u - 2 + s)
-                tile = r2[pl.ds(HALF * c + start, DEVS, ROWS), :]
-                if i == 0:
-                    inside = (lane128 >= LT * s) & (lane128 < LT * s + LT)
-                    tile = jnp.where(inside | (u > 0), tile, 0.0)
-                cols_s = slice(128 * s, 128 * s + 128)
-                rth[rows_u, cols_s], rtl[rows_u, cols_s] = split(tile.T)
-
-        @pl.when(j < 3)
-        def _():
-            def adjoint(n, inner):
-                cols = pl.ds(pl.multiple_of(256 * n, 256), 256)
-                y = dot3_deep(rth[rows, :], rtl[rows, :], th[part, cols], tl[part, cols])
-                gf[rows, cols] = jnp.where(c == 0, y, gf[rows, cols] + y)
-                return inner
-
-            lax.fori_loop(0, LON // 256, adjoint, 0)
-
-        @pl.when(j == 2)
-        def _():
-            gf[0:40, :] = gf[0:40, :] + gf[40:80, :] + gf[80:120, :]
-            for index in range(4):
-                sent(index, s1, send1)
-            for index in range(3):
-                sent(index, s2, send2)
-
+                transpose(c, 3 * h + i, s)
+
+        def adjoint(n, inner):
+            cols = pl.ds(pl.multiple_of(256 * n, 256), 256)
+            y = dot3_deep(rth[rows, :], rtl[rows, :], th[part, cols], tl[part, cols])
+            gf[rows, cols] = jnp.where(c == 0, y, gf[rows, cols] + y)
+            return inner
+
+        lax.fori_loop(0, LON // 256, adjoint, 0)
         return carry
 
-    lax.fori_loop(0, 4, returned, 0)
-    sent(3, s2, send2)
+    lax.fori_loop(0, 3, returned, 0)
+    gf[0:40, :] = gf[0:40, :] + gf[40:80, :] + gf[80:120, :]
+    for index in range(1, 4):
+        sent(index, s1, send1)
+    sent(0, s1, send1, 4)
+    sent(4, s1, send1, 4)
+    for index in range(3):
+        sent(index, s2, send2)
+    arrive(3, r2, recv2, 4)
+    for u, s in ((3, 0), (3, 1), (3, 2), (4, 0), (4, 1)):
+        transpose(1, u, s)
+
+    def adjoint_tile(n, carry):
+        cols = pl.ds(pl.multiple_of(256 * n, 256), 256)
+        gf[384:512, cols] += dot3_deep(
+            rth[384:512, :], rtl[384:512, :], th[384:768, cols], tl[384:768, cols]
+        )
+        return carry
+
+    lax.fori_loop(0, LON // 256, adjoint_tile, 0)
+    sent(3, s2, send2, 4)
+    arrive(4, r2, recv2, 4)
+    for u, s in ((4, 2), (5, 0), (5, 1), (5, 2)):
+        transpose(1, u, s)
+    sent(4, s2, send2, 4)
 
 
 def finish(gf, th, tl, rth, rtl, out, rest, sem):
@@ -431,25 +492,25 @@
         copies.append(copy)
 
     write(gf.at[pl.ds(0, LT)], out.at[16], 0)
-    for p in range(6):
+    for p in range(9):
         write(gf.at[pl.ds(128 + LT * p, LT)], out.at[lax.rem(p - w + 16, 16)], 1 + p)
-    rest[0:16, :] = gf[368:384, :]
+    rest[0:24, :] = gf[488:512, :]
 
     def step(n, carry):
         cols = pl.ds(pl.multiple_of(256 * n, 256), 256)
-        rest[16:400, cols] = gf[384:768, cols] + dot3_deep(
-            rth[384:768, :], rtl[384:768, :], th[384:768, cols], tl[384:768, cols]
+        rest[24:280, cols] = gf[512:768, cols] + dot3_deep(
+            rth[512:768, :], rtl[512:768, :], th[384:768, cols], tl[384:768, cols]
         )
-        for p in range(6, 16):
+        for p in range(9, 16):
             pltpu.make_async_copy(
-                rest.at[pl.ds(LT * (p - 6), LT), cols],
+                rest.at[pl.ds(LT * (p - 9), LT), cols],
                 out.at[lax.rem(p - w + 16, 16), :, cols],
-                sem.at[7],
+                sem.at[10],
             ).start()
         return carry
 
     lax.fori_loop(0, LON // 256, step, 0)
-    pltpu.make_async_copy(rest, rest, sem.at[7]).wait()
+    pltpu.make_async_copy(rest, rest, sem.at[10]).wait()
     for copy in copies:
         copy.wait()
 
@@ -487,7 +548,7 @@
             pltpu.VMEM((768, 384), bf16),
             pltpu.VMEM((768, 384), bf16),
         ],
-        in_specs=[pl.BlockSpec(memory_space=pltpu.SMEM), hbm, vmem] + [hbm] * 7,
+        in_specs=[hbm] * 9,
         out_specs=[vmem] * 5,
         scratch_shapes=[
             pltpu.VMEM((768, LON), bf16),
@@ -513,18 +574,19 @@
             pltpu.VMEM((DEVS * SLOTS, 128), f32),
             pltpu.VMEM((DEVS * SLOTS, 128), f32),
             pltpu.VMEM((1, DEVS * SLOTS), jnp.int32),
-            dma((10,)),
-            dma((4,)),
-            dma((4,)),
-            dma((4,)),
-            dma((4,)),
+            pltpu.VMEM((1, LEVELS), f32),
+            dma((11,)),
+            dma((5,)),
+            dma((5,)),
+            dma((5,)),
+            dma((5,)),
         ],
         compiler_params=pltpu.CompilerParams(
             collective_id=0, has_side_effects=True, vmem_limit_bytes=48 << 20
         ),
         name="spectral_step",
     )(
-        wavenumbers, wavenumbers, damping.reshape(1, -1), jnp.asarray(circle_table()),
+        wavenumbers, damping.reshape(1, -1), jnp.asarray(circle_table()),
         modes_in, modes_out, jnp.asarray(order), jnp.asarray(order.T.copy()),
         grid_in.reshape(LV, LT, LON), legendre,
     )
@@ -534,8 +596,8 @@
         in_specs=[vmem] * 5,
         out_specs=hbm,
         scratch_shapes=[
-            pltpu.VMEM((400, LON), f32),
-            dma((8,)),
+            pltpu.VMEM((280, LON), f32),
+            dma((11,)),
         ],
         compiler_params=pltpu.CompilerParams(vmem_limit_bytes=40 << 20),
         name="finish",

time: 66 us -> 64.2 us (0.973)
  Pallas kernels: 65.9 us -> 64.1 us
    pallas_call x1, Pallas kernels: 62.8 us -> 61.5 us  [local(): pl.pallas_call(kernel, out_shape=[pltpu.VMEM((768, LON), f32), pltpu.VMEM...]
where the time goes in v4:
time: 64.2 us; the launch traced here: 64.1 us
  Pallas kernels  64.1 us (100%)
    pallas_call x1, Pallas kernels, local(): pl.pallas_call(kernel, out_shape=[pltpu.VMEM((768, LON), f32), pltpu.VMEM...  61.5 us
    pallas_call x1, Pallas kernels, local(): pl.pallas_call(finish, out_shape=jax.ShapeDtypeStruct((LV, LT, LON), f32)...  2.58 us

profile of v4, /device:TPU:1, one launch (start us, length us, event | category | flops | bytes accessed | tf_op | source)
XLA Modules:
  0.0 64.1 jit_solution(13155223208467688446)
XLA Ops:
  0.0 61.5 %spectral_step.1 = (f32[768,1280]{1,0:T(8,128)S(1)}, bf16[768,1280]{1,0:T(8,128)(2,1)S(1)}, bf16[768,1280]{1,0:T(8,128)(2,1)S(1)}, bf16[768,384]{1,0:T(8,128)(2,1)S(1)}, bf16[768,384]{1,0:T(8,128)(2,1)S(1)}) custom-call(s32[384]{0:T(512)} %waves.1, f32[1,136]{1,0:T(1,128)} %bitcast.4, f32[384,384]{1,0:T(8,128)} %constant.6.clone.circle, ...), custom_call_target="tpu_custom_call" | custom-call | tf_op jit(solution)/shard_map/spectral_step/pallas_call | solution.py:542
  61.5 2.6 %finish.1 = f32[17,40,1280]{2,1,0:T(8,128)} custom-call(f32[768,1280]{1,0:T(8,128)S(1)} %get-tuple-element.10.gf, bf16[768,1280]{1,0:T(8,128)(2,1)S(1)} %get-tuple-element.11.th, bf16[768,1280]{1,0:T(8,128)(2,1)S(1)} %get-tuple-element.12.tl, bf16[768,384]{1,0:T(8,128)(2,1)S(1)} %get-tuple-element.13.rth, bf16[768,384]{1,0:T(8,128)(2,1)S(1)} %get-tuple-element.14.rtl), custom_call_target="tpu_custom_call" | custom-call | tf_op jit(solution)/shard_map/finish/pallas_call | solution.py:593

commit v5 on v4

--- a/solution.py
+++ b/solution.py
@@ -181,9 +181,9 @@
     small[0].wait()
     top, rest = split(circle_v[...])
     rows3 = dot(chosen, top, NN) + dot(chosen, rest, NN)
-    near_cos[...] = rows3[:, 0:128]
-    near_sin[...] = rows3[:, 128:256]
-    far[...] = rows3[:, 256:384]
+    near_cos[0:slots, :] = rows3[:, 0:128]
+    near_sin[0:slots, :] = rows3[:, 128:256]
+    far[0:slots, :] = rows3[:, 256:384]
 
     def make_table(c):
         def table(s, carry):
@@ -556,10 +556,10 @@
             pltpu.VMEM((SLOTS * LAT, COEFF), f32),
             pltpu.VMEM((SLOTS * LAT, COEFF), bf16),
             pltpu.VMEM((SLOTS * LAT, COEFF), bf16),
-            pltpu.VMEM((2 * HALF, 128), f32),
-            pltpu.VMEM((2 * HALF, 128), f32),
-            pltpu.VMEM((2 * HALF, 128), f32),
-            pltpu.VMEM((2 * HALF, 128), f32),
+            pltpu.VMEM((2 * HALF + ROWS, 128), f32),
+            pltpu.VMEM((2 * HALF + ROWS, 128), f32),
+            pltpu.VMEM((2 * HALF + ROWS, 128), f32),
+            pltpu.VMEM((2 * HALF + ROWS, 128), f32),
             pltpu.VMEM((PAD, LAT), f32),
             pltpu.VMEM((128, LAT), f32),
             pltpu.VMEM((WAVES * 8, 128), f32),
@@ -570,9 +570,9 @@
             pltpu.VMEM((LEVELS, LEVELS), f32),
             pltpu.VMEM((LEVELS, PAD), f32),
             pltpu.VMEM((PAD, LEVELS), f32),
-            pltpu.VMEM((DEVS * SLOTS, 128), f32),
-            pltpu.VMEM((DEVS * SLOTS, 128), f32),
-            pltpu.VMEM((DEVS * SLOTS, 128), f32),
+            pltpu.VMEM((DEVS * SLOTS + 8, 128), f32),
+            pltpu.VMEM((DEVS * SLOTS + 8, 128), f32),
+            pltpu.VMEM((DEVS * SLOTS + 8, 128), f32),
             pltpu.VMEM((1, DEVS * SLOTS), jnp.int32),
             pltpu.VMEM((1, LEVELS), f32),
             dma((11,)),

time: 64.2 us -> 64.2 us (level)
  no operation moved by 1% of the time
where the time goes in v5:
time: 64.2 us; the launch traced here: 64.1 us
  Pallas kernels  64.1 us (100%)
    pallas_call x1, Pallas kernels, local(): pl.pallas_call(kernel, out_shape=[pltpu.VMEM((768, LON), f32), pltpu.VMEM...  61.5 us
    pallas_call x1, Pallas kernels, local(): pl.pallas_call(finish, out_shape=jax.ShapeDtypeStruct((LV, LT, LON), f32)...  2.58 us

profile of v5, /device:TPU:1, one launch (start us, length us, event | category | flops | bytes accessed | tf_op | source)
XLA Modules:
  0.0 64.1 jit_solution(5564284698861579331)
XLA Ops:
  0.0 61.5 %spectral_step.1 = (f32[768,1280]{1,0:T(8,128)S(1)}, bf16[768,1280]{1,0:T(8,128)(2,1)S(1)}, bf16[768,1280]{1,0:T(8,128)(2,1)S(1)}, bf16[768,384]{1,0:T(8,128)(2,1)S(1)}, bf16[768,384]{1,0:T(8,128)(2,1)S(1)}) custom-call(s32[384]{0:T(512)} %waves.1, f32[1,136]{1,0:T(1,128)} %bitcast.4, f32[384,384]{1,0:T(8,128)} %constant.6.clone.circle, ...), custom_call_target="tpu_custom_call" | custom-call | tf_op jit(solution)/shard_map/spectral_step/pallas_call | solution.py:542
  61.5 2.6 %finish.1 = f32[17,40,1280]{2,1,0:T(8,128)} custom-call(f32[768,1280]{1,0:T(8,128)S(1)} %get-tuple-element.10.gf, bf16[768,1280]{1,0:T(8,128)(2,1)S(1)} %get-tuple-element.11.th, bf16[768,1280]{1,0:T(8,128)(2,1)S(1)} %get-tuple-element.12.tl, bf16[768,384]{1,0:T(8,128)(2,1)S(1)} %get-tuple-element.13.rth, bf16[768,384]{1,0:T(8,128)(2,1)S(1)} %get-tuple-element.14.rtl), custom_call_target="tpu_custom_call" | custom-call | tf_op jit(solution)/shard_map/finish/pallas_call | solution.py:593

commit v6 on v5

--- a/solution.py
+++ b/solution.py
@@ -133,12 +133,6 @@
     v = lax.axis_index("lev")
     me = w * LEVS + v
 
-    barrier = pltpu.get_barrier_semaphore()
-
-    def greet(to_wave, to_lev):
-        pl.semaphore_signal(barrier, inc=1, device_id=(to_wave, to_lev), device_id_type=MESH)
-
-    each_peer(greet)
     small = [
         pltpu.make_async_copy(a, b, load_sem.at[2 + i if i < 5 else 10])
         for i, (a, b) in enumerate(
@@ -151,6 +145,13 @@
     row_copy = pltpu.make_async_copy(waves, waves_row.at[0], load_sem.at[7])
     row_copy.start()
     small[0].start()
+
+    barrier = pltpu.get_barrier_semaphore()
+
+    def greet(to_wave, to_lev):
+        pl.semaphore_signal(barrier, inc=1, device_id=(to_wave, to_lev), device_id_type=MESH)
+
+    each_peer(greet)
     for s in range(SLOTS):
         pltpu.make_async_copy(
             grid.at[16], gf.at[pl.ds(LT * s, LT)], load_sem.at[0]

time: 64.2 us -> 63.2 us (0.984)
  Pallas kernels: 64.1 us -> 63.1 us
    pallas_call x1, Pallas kernels: 61.5 us -> 60.5 us  [local(): pl.pallas_call(kernel, out_shape=[pltpu.VMEM((768, LON), f32), pltpu.VMEM...]
where the time goes in v6:
time: 63.2 us; the launch traced here: 63.1 us
  Pallas kernels  63.1 us (100%)
    pallas_call x1, Pallas kernels, local(): pl.pallas_call(kernel, out_shape=[pltpu.VMEM((768, LON), f32), pltpu.VMEM...  60.5 us
    pallas_call x1, Pallas kernels, local(): pl.pallas_call(finish, out_shape=jax.ShapeDtypeStruct((LV, LT, LON), f32)...  2.58 us

profile of v6, /device:TPU:1, one launch (start us, length us, event | category | flops | bytes accessed | tf_op | source)
XLA Modules:
  0.0 63.1 jit_solution(6868465898820873633)
XLA Ops:
  0.0 60.5 %spectral_step.1 = (f32[768,1280]{1,0:T(8,128)S(1)}, bf16[768,1280]{1,0:T(8,128)(2,1)S(1)}, bf16[768,1280]{1,0:T(8,128)(2,1)S(1)}, bf16[768,384]{1,0:T(8,128)(2,1)S(1)}, bf16[768,384]{1,0:T(8,128)(2,1)S(1)}) custom-call(s32[384]{0:T(512)} %waves.1, f32[1,136]{1,0:T(1,128)} %bitcast.4, f32[384,384]{1,0:T(8,128)} %constant.6.clone.circle, ...), custom_call_target="tpu_custom_call" | custom-call | tf_op jit(solution)/shard_map/spectral_step/pallas_call | solution.py:543
  60.5 2.6 %finish.1 = f32[17,40,1280]{2,1,0:T(8,128)} custom-call(f32[768,1280]{1,0:T(8,128)S(1)} %get-tuple-element.10.gf, bf16[768,1280]{1,0:T(8,128)(2,1)S(1)} %get-tuple-element.11.th, bf16[768,1280]{1,0:T(8,128)(2,1)S(1)} %get-tuple-element.12.tl, bf16[768,384]{1,0:T(8,128)(2,1)S(1)} %get-tuple-element.13.rth, bf16[768,384]{1,0:T(8,128)(2,1)S(1)} %get-tuple-element.14.rtl), custom_call_target="tpu_custom_call" | custom-call | tf_op jit(solution)/shard_map/finish/pallas_call | solution.py:594
